TPU v7x, 256 devices: a whole 4x4x8 slice. The times are simulated.
256 devices in a mesh: dom: 128 (over x, z, y), mp: 2 (over core).
Axes of the slice: x: 4, y: 4, z: 8, core: 2. Of those that a mesh axis runs over, the one named last changes fastest.
Arguments:
- node_feats: bfloat16 [32768, 1024], P('dom'), may hold values from -24 to 24
- proj_weight: bfloat16 [1024, 3, 1024], P(None, None, 'mp'), may hold values from -0.1875 to 0.1875
- norm_gain: float32 [2, 1024], P(None, 'mp'), may hold values from 0.25 to 1.75
- grad_out: bfloat16 [32768, 1024], P('dom', 'mp'), may hold values from -6 to 6
- tile_lists: int32 [256, 6], P('dom'), may hold values from 0 to 9, as said below
- tile_valid: int32 [256], P('dom'), may hold values from 1 to 128, as said below
- send_rows: int32 [16384, 8], P('dom'), may hold values from 0 to 255
- send_count: int32 [128, 128], P('dom'), may hold values from 1 to 8, as said below
Outputs:
- proj_grad: float32 [1024, 3, 1024], P('dom', None, 'mp')
- input_grad: bfloat16 [32768, 1024], P('dom', 'mp')
Inputs may be any that keep to these rules, and one draw needn't show every extreme that they name: `tile_lists`: entries below 2 name the partition's own tiles, the others name tiles of its received slots. `tile_valid`: at least one tile is full. `send_rows`: local row numbers in the sending partition; slots at or beyond the count are unused. `send_count`: row p, column d: the used slots from partition p to partition d; every partition fills all 8 slots to some peer.
All inputs are finite; a program needn't handle non-finite values.
Results may differ from a plain program's by a relative error of at most 0.015.
Values may be sent and summed in bfloat16 or wider, within the bound.
A program may use at most 128 MiB of HBM per device.

v0:
```python
import math

import jax
import jax.numpy as jnp
from jax import lax
from jax.sharding import PartitionSpec as P

DH = 64
TILE = 128


norm_eps = 1e-06


def rms_heads(raw_rows, gain_row, head_count):
    row_count, col_width = raw_rows.shape
    shaped = raw_rows.reshape(row_count, head_count, col_width // head_count)
    inverse = lax.rsqrt(jnp.mean(shaped * shaped, axis=2, keepdims=True) + norm_eps)
    return ((shaped * inverse).reshape(row_count, col_width) * gain_row, inverse)


def rms_back(raw_rows, inverse, gain_row, upstream, head_count):
    row_count, col_width = raw_rows.shape
    shaped = raw_rows.reshape(row_count, head_count, col_width // head_count)
    scaled = (upstream * gain_row).reshape(row_count, head_count, col_width // head_count)
    inner_mean = jnp.mean(shaped * scaled, axis=2, keepdims=True)
    result = inverse * scaled - shaped * (inverse * inverse * inverse) * inner_mean
    return result.reshape(row_count, col_width)


def project(node_feats, proj_weight, norm_gain, head_count):
    row_count = node_feats.shape[0]
    col_width = proj_weight.shape[2]
    flat_weight = proj_weight.reshape(proj_weight.shape[0], 3 * col_width)
    mixed_proj = jnp.dot(node_feats, flat_weight, preferred_element_type=jnp.float32).reshape(
        row_count, 3, col_width
    )
    q_hat, q_inverse = rms_heads(mixed_proj[:, 0], norm_gain[0], head_count)
    k_hat, k_inverse = rms_heads(mixed_proj[:, 1], norm_gain[1], head_count)
    return (
        q_hat.astype(jnp.bfloat16),
        k_hat.astype(jnp.bfloat16),
        mixed_proj[:, 2].astype(jnp.bfloat16),
        mixed_proj,
        q_inverse,
        k_inverse,
    )


def attend_back(q_hat, k_table, v_table, key_live, tile_lists, upstream, head_count):
    tile_count, list_len = tile_lists.shape
    table_tiles = k_table.shape[0] // TILE
    col_width = q_hat.shape[1]
    head_dim = col_width // head_count
    score_scale = 1.0 / math.sqrt(head_dim)
    key_tiles = k_table.reshape(table_tiles, TILE, col_width)
    value_tiles = v_table.reshape(table_tiles, TILE, col_width)
    live_tiles = key_live.reshape(table_tiles, TILE)
    query_tiles = q_hat.reshape(tile_count, TILE, head_count, head_dim)
    grad_tiles = upstream.reshape(tile_count, TILE, head_count, head_dim)

    def one_tile(carry, inputs):
        key_acc, value_acc = carry
        listed, queries, grad_rows = inputs
        key_rows = key_tiles[listed].reshape(list_len * TILE, head_count, head_dim)
        value_rows = value_tiles[listed].reshape(list_len * TILE, head_count, head_dim)
        live_rows = live_tiles[listed].reshape(1, 1, list_len * TILE)
        scores = (
            jnp.einsum("qhd,khd->hqk", queries, key_rows, preferred_element_type=jnp.float32)
            * score_scale
        )
        weights = jnp.where(live_rows, jnp.exp(scores), jnp.zeros_like(scores))
        prob_full = weights / jnp.sum(weights, axis=2, keepdims=True)
        prob_low = prob_full.astype(jnp.bfloat16)
        output = jnp.einsum(
            "hqk,khd->qhd", prob_low, value_rows, preferred_element_type=jnp.float32
        )
        row_delta = jnp.sum(grad_rows.astype(jnp.float32) * output, axis=2)
        grad_values = jnp.einsum(
            "hqk,qhd->khd", prob_low, grad_rows, preferred_element_type=jnp.float32
        )
        grad_probs = jnp.einsum(
            "qhd,khd->hqk", grad_rows, value_rows, preferred_element_type=jnp.float32
        )
        grad_scores = (
            prob_full * (grad_probs - jnp.transpose(row_delta, (1, 0))[:, :, None])
        ).astype(jnp.bfloat16)
        grad_queries = (
            jnp.einsum("hqk,khd->qhd", grad_scores, key_rows, preferred_element_type=jnp.float32)
            * score_scale
        )
        grad_keys = (
            jnp.einsum("hqk,qhd->khd", grad_scores, queries, preferred_element_type=jnp.float32)
            * score_scale
        )
        flat_width = TILE * col_width
        key_acc = key_acc.at[listed].add(grad_keys.reshape(list_len, flat_width))
        value_acc = value_acc.at[listed].add(grad_values.reshape(list_len, flat_width))
        return ((key_acc, value_acc), grad_queries.reshape(TILE, col_width))

    zero_table = jnp.zeros((table_tiles, TILE * col_width), jnp.float32)
    (key_table_grad, value_table_grad), grad_queries = lax.scan(
        one_tile, (zero_table, zero_table), (tile_lists, query_tiles, grad_tiles)
    )
    return (
        grad_queries.reshape(tile_count * TILE, col_width),
        key_table_grad.reshape(table_tiles * TILE, col_width),
        value_table_grad.reshape(table_tiles * TILE, col_width),
    )


def body(
    node_feats, proj_weight, norm_gain, grad_out, tile_lists, tile_valid, send_rows, send_count
):
    rows_dev, model_width = node_feats.shape
    col_width = proj_weight.shape[2]
    head_count = col_width // DH
    slot_cap = send_rows.shape[1]
    flat_rows = send_rows.reshape(-1)
    q_hat, k_hat, values, mixed_proj, q_inverse, k_inverse = project(
        node_feats, proj_weight, norm_gain, head_count
    )
    outgoing = jnp.concatenate([k_hat[flat_rows], values[flat_rows]], axis=1)
    arrived = lax.all_to_all(outgoing, "dom", split_axis=0, concat_axis=0, tiled=True)
    far_keys = arrived[:, :col_width]
    far_values = arrived[:, col_width:]
    arrived_counts = lax.all_to_all(send_count, "dom", split_axis=1, concat_axis=0, tiled=True)
    slot_live = (jnp.arange(slot_cap, dtype=jnp.int32)[None, :] < arrived_counts).reshape(-1)
    own_live = (jnp.arange(TILE, dtype=jnp.int32)[None, :] < tile_valid[:, None]).reshape(-1)
    k_table = jnp.concatenate([k_hat, far_keys], axis=0)
    v_table = jnp.concatenate([values, far_values], axis=0)
    key_live = jnp.concatenate([own_live, slot_live], axis=0)
    query_hat_grad, key_table_grad, value_table_grad = attend_back(
        q_hat, k_table, v_table, key_live, tile_lists, grad_out, head_count
    )
    back_rows = jnp.concatenate([key_table_grad[rows_dev:], value_table_grad[rows_dev:]], axis=1)
    returned = lax.all_to_all(
        back_rows.astype(jnp.bfloat16), "dom", split_axis=0, concat_axis=0, tiled=True
    ).astype(back_rows.dtype)
    key_total = key_table_grad[:rows_dev].at[flat_rows].add(returned[:, :col_width])
    value_total = value_table_grad[:rows_dev].at[flat_rows].add(returned[:, col_width:])
    query_grad = rms_back(mixed_proj[:, 0], q_inverse, norm_gain[0], query_hat_grad, head_count)
    key_grad = rms_back(mixed_proj[:, 1], k_inverse, norm_gain[1], key_total, head_count)
    grads_low = jnp.stack([query_grad, key_grad, value_total], axis=1).astype(jnp.bfloat16)
    grads_low = grads_low.reshape(rows_dev, 3 * col_width)
    flat_weight = proj_weight.reshape(model_width, 3 * col_width)
    grad_term = lax.dot_general(
        node_feats, grads_low, (((0,), (0,)), ((), ())), preferred_element_type=jnp.float32
    ).reshape(model_width, 3, col_width)
    proj_grad = lax.psum_scatter(grad_term, "dom", scatter_dimension=0, tiled=True)
    input_term = lax.dot_general(
        grads_low, flat_weight, (((1,), (1,)), ((), ())), preferred_element_type=jnp.float32
    )
    input_whole = lax.psum(input_term.astype(jnp.bfloat16), "mp").astype(jnp.float32)
    half_cols = model_width // lax.axis_size("mp")
    input_grad = lax.dynamic_slice_in_dim(
        input_whole, lax.axis_index("mp") * half_cols, half_cols, 1
    )
    return (proj_grad, input_grad.astype(jnp.bfloat16))


def solution(mesh):
    in_specs = (
        P("dom", None),
        P(None, None, "mp"),
        P(None, "mp"),
        P("dom", "mp"),
        P("dom", None),
        P("dom"),
        P("dom", None),
        P("dom", None),
    )
    out_specs = (P("dom", None, "mp"), P("dom", "mp"))
    return jax.shard_map(body, mesh=mesh, in_specs=in_specs, out_specs=out_specs, check_vma=False)
```

profile of v0, /device:TPU:32, one launch (start us, length us, event | category | flops | bytes accessed | tf_op | source)
XLA Modules:
  0.0 1074.6 jit_solution(15584772968659953902)
XLA Ops:
  9.5 15.0 %all-to-all-start = ((s32[1,128,1]{2,0,1:T(1,128)}), s32[1,128,1]{2,0,1:T(1,128)S(1)}, u32[]{:S(2)}, u32[]{:S(2)}) async-start(s32[1,128,1]{2,0,1:T(1,128)} %copy.76), calls=%async_computation | async-start | bytes 131072 | tf_op jit(solution)/shard_map/all_to_all | solution.py:127
  24.5 4.7 copy.72
  29.1 2.9 fusion.23
  38.3 5.1 gather_fusion.3
  43.4 5.1 gather_fusion.4
  48.4 2.8 maximum_bitcast_fusion
  51.3 13.9 %all-to-all-start.1 = ((bf16[128,8,1024]{2,1,0:T(8,128)(2,1)}), bf16[128,8,1024]{2,1,0:T(8,128)(2,1)S(1)}, u32[]{:S(2)}, u32[]{:S(2)}) async-start(bf16[128,8,1024]{2,1,0:T(8,128)(2,1)} %maximum_bitcast_fusion), calls=%async_computation.1 | async-start | bytes 4194304 | tf_op jit(solution)/shard_map/all_to_all | solution.py:124
  65.2 2.1 copy.73
  67.3 2.1 reshape_squeeze.13
  74.7 2.0 copy.82
  76.8 2.3 reduce.1
  79.3 37.9 %all-to-all-done.1 = bf16[128,8,1024]{2,1,0:T(8,128)(2,1)S(1)} async-done(((bf16[128,8,1024]{2,1,0:T(8,128)(2,1)}), bf16[128,8,1024]{2,1,0:T(8,128)(2,1)S(1)}, u32[]{:S(2)}, u32[]{:S(2)}) %all-to-all-start.1) | async-done | bytes 2097184 | tf_op jit(solution)/shard_map/all_to_all | solution.py:124
  119.0 2.2 broadcast_in_dim.14
  121.3 2.2 broadcast_in_dim.14.clone
  123.5 141.6 %while.14 = (s32[]{:T(128)}, f32[10,65536]{1,0:T(8,128)}, f32[10,65536]{1,0:T(8,128)}, f32[2,128,512]{1,2,0:T(8,128)}, s32[2,6]{1,0:T(2,128)S(1)}, /*index=5*/bf...) while((s32[]{:T(128)}, f32[10,65536]{1,0:T(8,128)}, ...), condition=%wide.region_7.8_spmd, body=%wide.region_2.7_spmd.sunk | while | flops 618789888 | bytes 91130600 | solution.py:102
  138.8 1.9 gather_fusion.2
  142.4 1.8 fusion.77
  144.2 1.7 copy-done.29
  145.9 1.8 convolution_bitcast_fusion.4
  147.6 2.3 copy.103
  150.0 2.9 reshape.413
  152.8 15.9 %scatter_fusion.1 = f32[10,65536]{1,0:T(8,128)} fusion(f32[10,65536]{1,0:T(8,128)} %get-tuple-element.205, s32[6]{0:T(128)S(1)} %fusion.76, f32[6,65536]{1,0:T(8,128)S(1)} %reshape.413), kind=kCustom, calls=%fused_computation.6.clone.1 | custom fusion | flops 393216 | bytes 4718616 | tf_op jit(solution)/shard_map/while/body/eval_jaxpr/scatter-add | solution.py:98
  168.8 2.0 gather_fusion
  172.4 2.9 fusion.78
  178.1 2.3 copy.102
  180.4 2.9 reshape.412
  183.3 15.8 %scatter_fusion = f32[10,65536]{1,0:T(8,128)} fusion(f32[10,65536]{1,0:T(8,128)} %get-tuple-element.204, s32[6]{0:T(128)S(1)} %fusion.76, f32[6,65536]{1,0:T(8,128)S(1)} %reshape.412), kind=kCustom, calls=%fused_computation.5.clone.1 | custom fusion | flops 393216 | bytes 4718616 | tf_op jit(solution)/shard_map/while/body/eval_jaxpr/scatter-add | solution.py:97
  199.1 2.1 convolution_multiply_fusion.2
  202.5 1.9 gather_fusion.2
  206.0 1.8 fusion.77
  207.8 1.7 copy-done.29
  209.5 1.8 convolution_bitcast_fusion.4
  211.3 2.3 copy.103
  213.6 2.9 reshape.413
  216.5 15.7 %scatter_fusion.1 = f32[10,65536]{1,0:T(8,128)} fusion(f32[10,65536]{1,0:T(8,128)} %get-tuple-element.205, s32[6]{0:T(128)S(1)} %fusion.76, f32[6,65536]{1,0:T(8,128)S(1)} %reshape.413), kind=kCustom, calls=%fused_computation.6.clone.1 | custom fusion | flops 393216 | bytes 4718616 | tf_op jit(solution)/shard_map/while/body/eval_jaxpr/scatter-add | solution.py:98
  232.2 2.0 gather_fusion
  235.9 2.9 fusion.78
  241.5 2.3 copy.102
  243.9 2.9 reshape.412
  246.7 15.6 %scatter_fusion = f32[10,65536]{1,0:T(8,128)} fusion(f32[10,65536]{1,0:T(8,128)} %get-tuple-element.204, s32[6]{0:T(128)S(1)} %fusion.76, f32[6,65536]{1,0:T(8,128)S(1)} %reshape.412), kind=kCustom, calls=%fused_computation.5.clone.1 | custom fusion | flops 393216 | bytes 4718616 | tf_op jit(solution)/shard_map/while/body/eval_jaxpr/scatter-add | solution.py:97
  262.4 2.1 convolution_multiply_fusion.2
  265.1 2.4 slice.105
  268.0 2.4 slice.104
  271.8 2.8 pad_maximum_fusion
  274.7 7.5 all-to-all-start.2
  285.4 2.6 slice.64
  288.0 2.2 copy.86
  290.2 2.1 copy.83
  292.3 2.5 slice.69
  294.8 2.3 slice.65
  297.1 2.3 reshape.295
  301.6 2.3 slice.70
  303.9 29.5 %all-to-all-done.2 = bf16[128,8,1024]{2,1,0:T(8,128)(2,1)S(1)} async-done(((bf16[128,8,1024]{2,1,0:T(8,128)(2,1)}), bf16[128,8,1024]{2,1,0:T(8,128)(2,1)S(1)}, u32[]{:S(2)}, u32[]{:S(2)}) %all-to-all-start.2) | async-done | bytes 2097184 | tf_op jit(solution)/shard_map/all_to_all | solution.py:137
  333.4 2.4 bitcast_convert_fusion
  335.8 7.6 scatter_custom_fusion.2
  344.4 2.2 copy.90
  348.7 2.0 copy.91
  350.7 9.4 scatter_custom_fusion.3
  360.1 2.6 fusion.31
  363.1 1.8 fusion.29
  365.3 3.6 fusion.40
  369.0 6.6 copy.93
  375.6 13.9 %all-reduce.2.cloned.1.call-done = bf16[256,1024]{1,0:T(8,128)(2,1)} async-done(((bf16[256,1024]{1,0:T(8,128)(2,1)}), bf16[256,1024]{1,0:T(8,128)(2,1)}) %all-reduce.2.cloned.1.call-update) | async-done | bytes 524304 | tf_op jit(solution)/shard_map/psum | solution.py:154
  391.2 675.7 %reduce-scatter.2.cloned.1.call-done = f32[8,3,512]{2,0,1:T(8,128)} async-done(((f32[1024,3,512]{2,0,1:T(8,128)}), f32[8,3,512]{2,0,1:T(8,128)}) %reduce-scatter.2.cloned.1.call-update) | async-done | bytes 49168 | tf_op jit(solution)/shard_map/reduce_scatter | solution.py:150
  (144 shorter events, 42.3 us)
Async XLA Ops:
  8.0 21.1 %copy-start = (bf16[256,1024]{1,0:T(8,128)(2,1)S(1)}, bf16[256,1024]{1,0:T(8,128)(2,1)}, u32[]{:S(2)}) copy-start(bf16[256,1024]{1,0:T(8,128)(2,1)} %param.10) | copy-start | bytes 1572868
  9.5 41.8 %all-to-all-start = ((s32[1,128,1]{2,0,1:T(1,128)}), s32[1,128,1]{2,0,1:T(1,128)S(1)}, u32[]{:S(2)}, u32[]{:S(2)}) async-start(s32[1,128,1]{2,0,1:T(1,128)} %copy.76), calls=%async_computation | async-start | bytes 131072 | tf_op jit(solution)/shard_map/all_to_all | solution.py:127
  32.0 6.2 copy-start.2
  32.1 5.2 copy-start.26
  32.1 5.9 copy-start.25
  34.4 1.6 copy-start.8
  37.3 6.0 copy-start.5
  37.9 5.4 copy-start.18
  38.2 5.2 copy-start.23
  43.4 5.1 copy-start.9
  51.3 22.3 %copy-start.13 = (bf16[256,512]{1,0:T(8,128)(2,1)S(1)}, bf16[256,512]{1,0:T(8,128)(2,1)}, u32[]{:S(2)}) copy-start(bf16[256,512]{1,0:T(8,128)(2,1)} %param.13) | copy-start | bytes 786436
  51.3 66.0 %all-to-all-start.1 = ((bf16[128,8,1024]{2,1,0:T(8,128)(2,1)}), bf16[128,8,1024]{2,1,0:T(8,128)(2,1)S(1)}, u32[]{:S(2)}, u32[]{:S(2)}) async-start(bf16[128,8,1024]{2,1,0:T(8,128)(2,1)} %maximum_bitcast_fusion), calls=%async_computation.1 | async-start | bytes 4194304 | tf_op jit(solution)/shard_map/all_to_all | solution.py:124
  65.2 11.5 %copy-start.28 = (s32[2]{0:T(128)S(1)}, s32[2]{0:T(128)}, u32[]{:S(2)}) copy-start(s32[2]{0:T(128)} %param.15) | copy-start | bytes 28
  71.2 46.2 %copy-start.16 = (f32[8,64]{1,0:T(8,128)}, f32[8,64]{1,0:T(8,128)S(1)}, u32[]{:S(2)}) copy-start(f32[8,64]{1,0:T(8,128)S(1)} %mul.232) | copy-start | bytes 6148
  121.3 2.2 copy-start.27
  144.1 1.7 copy-start.29
  168.8 3.6 copy-start.14
  172.4 3.0 copy-start.15
  172.4 3.0 copy-start.30
  175.4 2.3 copy-start.10
  176.5 1.2 copy-start.1
  207.8 1.7 copy-start.29
  232.2 3.6 copy-start.14
  235.9 3.0 copy-start.15
  235.9 3.0 copy-start.30
  238.8 2.3 copy-start.10
  239.9 1.2 copy-start.1
  274.7 7.5 copy-start.22
  274.7 8.6 copy-start.21
  274.7 9.6 copy-start.20
  274.7 58.7 %all-to-all-start.2 = ((bf16[128,8,1024]{2,1,0:T(8,128)(2,1)}), bf16[128,8,1024]{2,1,0:T(8,128)(2,1)S(1)}, u32[]{:S(2)}, u32[]{:S(2)}) async-start(bf16[128,8,1024]{2,1,0:T(8,128)(2,1)} %pad_maximum_fusion), calls=%async_computation.2 | async-start | bytes 4194304 | tf_op jit(solution)/shard_map/all_to_all | solution.py:137
  282.2 107.3 %all-reduce.2.cloned.1.call-start = ((), (), s32[]{:S(2)}) async-start(), calls=%async_computation.5 | async-start | bytes 1048576 | tf_op jit(solution)/shard_map/psum | solution.py:154
  285.4 14.0 %copy-start.4 = (f32[256,1,512]{0,2,1:T(8,128)S(1)}, f32[256,1,512]{0,2,1:T(8,128)}, u32[]{:S(2)}) copy-start(f32[256,1,512]{0,2,1:T(8,128)} %copy.73) | copy-start | bytes 1572868
  285.4 14.0 %copy-start.17 = (f32[8,64]{1,0:T(8,128)S(1)}, f32[8,64]{1,0:T(8,128)}, u32[]{:S(2)}) copy-start(f32[8,64]{1,0:T(8,128)} %copy-done.16) | copy-start | bytes 6148
  303.9 31.9 %copy-start.7 = (f32[256,512]{1,0:T(8,128)S(1)}, f32[256,512]{1,0:T(8,128)}, u32[]{:S(2)}) copy-start(f32[256,512]{1,0:T(8,128)} %slice.65) | copy-start | bytes 1572868
  303.9 39.5 %copy-start.19 = (f32[1,512]{1,0:T(1,128)S(1)}, f32[1,512]{1,0:T(1,128)}, u32[]{:S(2)}) copy-start(f32[1,512]{1,0:T(1,128)} %copy-done.18) | copy-start | bytes 6148
  344.4 15.8 %copy-start.3 = (f32[256,3,512]{2,0,1:T(8,128)S(1)}, f32[256,3,512]{2,0,1:T(8,128)}, u32[]{:S(2)}) copy-start(f32[256,3,512]{2,0,1:T(8,128)} %copy-done.2) | copy-start | bytes 4718596
  344.4 15.8 %copy-start.6 = (f32[256,512]{1,0:T(8,128)S(1)}, f32[256,512]{1,0:T(8,128)}, u32[]{:S(2)}) copy-start(f32[256,512]{1,0:T(8,128)} %copy-done.5) | copy-start | bytes 1572868
  344.4 15.8 %copy-start.24 = (f32[1,512]{1,0:T(1,128)S(1)}, f32[1,512]{1,0:T(1,128)}, u32[]{:S(2)}) copy-start(f32[1,512]{1,0:T(1,128)} %get-tuple-element.122) | copy-start | bytes 6148
  360.1 2.7 copy-start.12
  360.1 3.0 copy-start.11
  365.0 701.9 %reduce-scatter.2.cloned.1.call-start = ((), (), s32[]{:S(2)}) async-start(), calls=%async_computation.4 | async-start | bytes 6340608 | tf_op jit(solution)/shard_map/reduce_scatter | solution.py:150
Sparse Core Ops, SparseCore 0:
  365.1 24.3 all-reduce.1
Sparse Core Ops, SparseCore 1:
  375.6 691.2 reduce-scatter.1
where the time goes:
time: 1090 us; the launch traced here: 1070 us
  waiting for transfers between devices  757 us (69%)
  local copies, waits for them, and re-layouts  117 us (11%)
  other arithmetic  104 us (10%)
  starting transfers between devices  36.5 us (3%)
  matrix products  28.3 us (3%)
  between operations  16.1 us (1%)
  loops' own time  15 us (1%)
    reduce_scatter x1, waiting for transfers between devices, body(): lax.psum_scatter(grad_term, 'dom', scatter_dimension=0, tiled=True)  676 us
    all_to_all x1, waiting for transfers between devices, body(): lax.all_to_all(outgoing, 'dom', split_axis=0, concat_axis=0, tiled=True)  37.9 us
    scatter-add x2, other arithmetic, one_tile(): value_acc.at[listed].add(grad_values.reshape(list_len, flat_width))  31.6 us
    scatter-add x2, other arithmetic, one_tile(): key_acc = key_acc.at[listed].add(grad_keys.reshape(list_len, flat_width))  31.4 us
    all_to_all x1, waiting for transfers between devices, body(): lax.all_to_all(back_rows.astype(jnp.bfloat16), 'dom', split_axis=0, conca...  29.5 us
  transfers between devices with their start and end apart: 5, of which 4 were waited for; matrix products, arithmetic and copies ran while one was open for 7% of the time, Pallas kernels for 0%

commit v1 on v0

v1 whole, which is shorter than its diff:
```python
import math

import jax
import jax.numpy as jnp
from jax import lax
from jax.experimental import pallas as pl
from jax.experimental.pallas import tpu as pltpu
from jax.sharding import PartitionSpec as P

DH = 64
TILE = 128
CAP = 8
SLAB = 2 * CAP
EPS = 1e-06
AX, AZ, AY = 4, 8, 4
N = AX * AZ * AY
DEAD = 1024.0
LIVE_MAX = 512.0
LOG2E = math.log2(math.e)
MESH = pl.DeviceIdType.MESH
F32 = jnp.float32
BF16 = jnp.bfloat16


def dot(a, b):
    return jnp.dot(a, b, preferred_element_type=F32)


def dot_nt(a, b):
    return lax.dot_general(a, b, (((1,), (1,)), ((), ())), preferred_element_type=F32)


def dot_tn(a, b):
    return lax.dot_general(a, b, (((0,), (0,)), ((), ())), preferred_element_type=F32)


def place():
    dom = lax.axis_index("dom")
    core = lax.axis_index("mp")
    return dom, core, dom // (AZ * AY), lax.rem(dom // AY, AZ), lax.rem(dom, AY)


def rows_at(start, size):
    return pl.ds(pl.multiple_of(start, SLAB), size)


def greet_all(dom, core):
    barrier = pltpu.get_barrier_semaphore()

    def greet(i, carry):
        peer = lax.rem(dom + 1 + i, N)
        pl.semaphore_signal(barrier, inc=1, device_id={"dom": peer}, device_id_type=MESH)
        return carry

    lax.fori_loop(0, N - 1, greet, 0)
    pl.semaphore_signal(barrier, inc=1, device_id={"mp": 1 - core}, device_id_type=MESH)
    return barrier


def wait_bytes(ref, sem):
    pltpu.make_async_copy(ref, ref, sem).wait()


def push_block(step, mine, src, dst, send_sem, recv_sem):
    dom, core, x, z, y = mine
    far = lax.rem(x + step, AX)

    def push(i, carry):
        dz, dy = i // AY, lax.rem(i, AY)
        peer = far * (AZ * AY) + lax.rem(z + dz, AZ) * AY + lax.rem(y + dy, AY)
        pltpu.make_async_remote_copy(
            src_ref=src.at[rows_at(peer * SLAB, SLAB)],
            dst_ref=dst.at[rows_at(dom * SLAB, SLAB)],
            send_sem=send_sem,
            recv_sem=recv_sem.at[step],
            device_id={"dom": peer},
            device_id_type=MESH,
        ).start()
        return carry

    lax.fori_loop(1 if step == 0 else 0, AZ * AY, push, 0)


BLOCK = AZ * AY * SLAB
BLOCK_KEYS = AZ * AY * CAP


def fetch_kernel(
    idx_ref, feats_ref, table_ref, halves, outgoing, landed, send_sem, recv_sem, pair_send, pair_recv
):
    mine = place()
    dom, core, x, z, y = mine
    barrier = greet_all(dom, core)
    rows, width = feats_ref.shape
    half = width // 2
    quarter = half // 2
    halves[0:rows, :] = feats_ref[:, pl.ds(pl.multiple_of(core * half, half), quarter)]
    halves[rows : 2 * rows, :] = feats_ref[
        :, pl.ds(pl.multiple_of(core * half + quarter, quarter), quarter)
    ]
    halves[2 * rows :, :] = jnp.full((SLAB, quarter), DEAD, BF16)
    for step in range(AX):
        far = lax.rem(x + step, AX)
        wanted = idx_ref[far]
        kinds = lax.broadcasted_iota(jnp.int32, (2 * rows + SLAB, BLOCK), 0)
        pick = jnp.where(kinds == wanted, 1.0, 0.0).astype(BF16)
        outgoing[rows_at(far * BLOCK, BLOCK), :] = dot_tn(pick, halves[...]).astype(BF16)
        if step == 0:
            pl.semaphore_wait(barrier, N)
        push_block(step, mine, outgoing, landed.at[core], send_sem, recv_sem)
    own = rows_at(dom * SLAB, SLAB)
    landed[core, own, :] = outgoing[own, :]
    pairs = []
    for step in range(AX):
        near = lax.rem(x - step + AX, AX)
        part = landed.at[core, rows_at(near * BLOCK, BLOCK)]
        if step == 0:
            wait_bytes(landed.at[core, pl.ds(0, BLOCK - SLAB)], recv_sem.at[step])
        else:
            wait_bytes(part, recv_sem.at[step])
        pair = pltpu.make_async_remote_copy(
            src_ref=part,
            dst_ref=part,
            send_sem=pair_send.at[step],
            recv_sem=pair_recv.at[step],
            device_id={"mp": 1 - core},
            device_id_type=MESH,
        )
        pair.start()
        pairs.append(pair)
    for step in range(AX):
        near = lax.rem(x - step + AX, AX)
        pairs[step].wait()
        keys = rows_at(near * BLOCK_KEYS, BLOCK_KEYS)
        for plane in range(2):
            slabs = landed[plane, rows_at(near * BLOCK, BLOCK), :].astype(F32)
            slabs = slabs.reshape(AZ * AY, SLAB, quarter)
            for side in range(2):
                columns = pl.ds(plane * half + side * quarter, quarter)
                block = slabs[:, side * CAP : (side + 1) * CAP, :].reshape(BLOCK_KEYS, quarter)
                table_ref[keys, columns] = block.astype(BF16)
    sent = outgoing.at[pl.ds(0, (N - 1) * SLAB)]
    wait_bytes(sent, send_sem)


def fetch(idx, feats):
    rows, width = feats.shape
    quarter = width // 4
    return pl.pallas_call(
        fetch_kernel,
        out_shape=jax.ShapeDtypeStruct((N * CAP, width), BF16),
        in_specs=[pl.BlockSpec(memory_space=pltpu.VMEM)] * 2,
        out_specs=pl.BlockSpec(memory_space=pltpu.VMEM),
        scratch_shapes=[
            pltpu.VMEM((2 * rows + SLAB, quarter), BF16),
            pltpu.VMEM((N * SLAB, quarter), BF16),
            pltpu.VMEM((2, N * SLAB, quarter), BF16),
            pltpu.SemaphoreType.DMA,
            pltpu.SemaphoreType.DMA((AX,)),
            pltpu.SemaphoreType.DMA((AX,)),
            pltpu.SemaphoreType.DMA((AX,)),
        ],
        compiler_params=pltpu.CompilerParams(
            collective_id=0, has_side_effects=True, vmem_limit_bytes=40 * 1024 * 1024
        ),
        name="fetch",
    )(idx, feats)


def slabbed(block, width):
    count = block.shape[0] // CAP
    left = block[:, :width].reshape(count, CAP, width)
    right = block[:, width:].reshape(count, CAP, width)
    return jnp.concatenate([left, right], axis=1).reshape(count * SLAB, width)


def layer_kernel(
    lists_ref,
    valid_ref,
    feats_ref,
    table_ref,
    weight_ref,
    gain_ref,
    grad_ref,
    first_ref,
    second_ref,
    keep_ref,
    send_ref,
    feats_t,
    k_hat,
    k_hat_t,
    k_unit,
    k_inv,
    values,
    q_unit,
    q_inv,
    q_t,
    g_t,
    mask_t,
    expo,
    expo_dp,
    dq_t,
    dk_sum,
    dv_sum,
    dk_low,
    dv_low,
):
    core = lax.axis_index("mp")
    rows, width = feats_ref.shape
    cols = grad_ref.shape[1]
    keys = k_hat.shape[0]
    blocks = keys // rows
    pairs = cols // (2 * DH)

    def feats_block(b):
        if b == 0:
            return feats_ref[...]
        return table_ref[(b - 1) * rows : b * rows, :]

    head_of = lax.broadcasted_iota(jnp.int32, (cols, cols), 0) // DH
    head_to = lax.broadcasted_iota(jnp.int32, (cols, cols), 1) // DH
    head_mean = jnp.where(head_of == head_to, 1.0 / DH, 0.0).astype(BF16)

    mixed_q = dot(feats_ref[...], weight_ref[0])
    inv = lax.rsqrt(dot((mixed_q * mixed_q).astype(BF16), head_mean) + EPS)
    unit = mixed_q * inv
    q_inv[...] = inv
    q_unit[...] = unit
    q_scaled = unit * (gain_ref[0:1, :] * (LOG2E / math.sqrt(DH)))
    q_t[...] = q_scaled.T
    g_t[...] = grad_ref[...].astype(F32).T

    for b in range(blocks):
        part = pl.ds(b * rows, rows)
        block = feats_block(b)
        feats_t[:, part] = block.T
        mixed_k = dot(block, weight_ref[1])
        inv = lax.rsqrt(dot((mixed_k * mixed_k).astype(BF16), head_mean) + EPS)
        unit = mixed_k * inv
        k_inv[part, :] = inv
        k_unit[part, :] = unit
        low = (unit * gain_ref[1:2, :]).astype(BF16)
        k_hat[part, :] = low
        k_hat_t[:, part] = low.T
        values[part, :] = dot(block, weight_ref[2]).astype(BF16)

    place_in_tile = lax.broadcasted_iota(jnp.int32, (TILE, TILE), 0)
    for j in range(keys // TILE):
        if j < rows // TILE:
            live = jnp.where(place_in_tile < valid_ref[j], 1.0, 0.0)
        else:
            at = (j - rows // TILE) * TILE
            mark = table_ref[at : at + TILE, 0:TILE].astype(F32)[:, 0:1]
            live = jnp.where(jnp.broadcast_to(mark, (TILE, TILE)) < LIVE_MAX, 1.0, 0.0)
        for t in range(rows // TILE):
            listed = jnp.int32(0)
            for i in range(lists_ref.shape[1]):
                listed += jnp.where(lists_ref[t, i] == j, 1, 0)
            mask_t[j * TILE : (j + 1) * TILE, t * TILE : (t + 1) * TILE] = live * listed.astype(F32)

    which = lax.broadcasted_iota(jnp.int32, (2 * DH, rows), 0) // DH

    def head_pair(pair, carry):
        lanes = pl.ds(pl.multiple_of(pair * 2 * DH, 2 * DH), 2 * DH)
        q_pair = q_t[lanes, :]
        g_pair = g_t[lanes, :]
        for h in range(2):
            q_h = jnp.where(which == h, q_pair, 0.0)
            g_h = jnp.where(which == h, g_pair, 0.0)
            q_low = q_h.astype(BF16)
            g_low = g_h.astype(BF16)
            total = jnp.zeros((1, rows), F32)
            moment = jnp.zeros((1, rows), F32)
            for b in range(blocks):
                part = pl.ds(b * rows, rows)
                e = jnp.exp2(dot(k_hat[part, lanes], q_low)) * mask_t[part, :]
                e_dp = e * dot(values[part, lanes], g_low)
                total += jnp.sum(e, axis=0, keepdims=True)
                moment += jnp.sum(e_dp, axis=0, keepdims=True)
                expo[h, part, :] = e
                expo_dp[h, part, :] = e_dp
            over = 1.0 / total
            delta = moment * over
            q_over = (q_h * (over * (1.0 / LOG2E))).astype(BF16)
            g_over = (g_h * over).astype(BF16)
            dq_h = jnp.zeros((DH, rows), F32)
            head_rows = pl.ds(pl.multiple_of(pair * 2 * DH + h * DH, DH), DH)
            for b in range(blocks):
                part = pl.ds(b * rows, rows)
                e = expo[h, part, :]
                ds = (expo_dp[h, part, :] - e * delta).astype(BF16)
                dv = dot_nt(e.astype(BF16), g_over)
                dk = dot_nt(ds, q_over)
                dq_h += dot(k_hat_t[head_rows, part], ds)
                if h == 0:
                    dv_sum[part, lanes] = dv
                    dk_sum[part, lanes] = dk
                else:
                    dv_sum[part, lanes] += dv
                    dk_sum[part, lanes] += dk
            dq_t[head_rows, :] = dq_h * (over * (1.0 / math.sqrt(DH)))
        return carry

    lax.fori_loop(0, pairs, head_pair, 0)

    def norm_back(unit, inv, upstream):
        inner = dot((unit * upstream).astype(BF16), head_mean)
        return inv * (upstream - unit * inner)

    dq_low = norm_back(q_unit[...], q_inv[...], dq_t[...].T * gain_ref[0:1, :]).astype(BF16)
    for b in range(blocks):
        part = pl.ds(b * rows, rows)
        upstream = dk_sum[part, :] * gain_ref[1:2, :]
        dk_low[part, :] = norm_back(k_unit[part, :], k_inv[part, :], upstream).astype(BF16)
        dv_low[part, :] = dv_sum[part, :].astype(BF16)

    half = width // 2
    for target, near in ((send_ref, 1 - core), (keep_ref, core)):
        wanted = pl.ds(pl.multiple_of(near * half, half), half)
        w_q, w_k, w_v = (weight_ref[c, wanted, :] for c in range(3))
        for b in range(blocks):
            part = pl.ds(b * rows, rows)
            term = dot_nt(dk_low[part, :], w_k) + dot_nt(dv_low[part, :], w_v)
            if b == 0:
                term += dot_nt(dq_low, w_q)
                first = N * SLAB
                target[first : first + rows, :] = term[:, : half // 2].astype(BF16)
                target[first + rows : first + 2 * rows, :] = term[:, half // 2 :].astype(BF16)
            else:
                target[(b - 1) * BLOCK : b * BLOCK, :] = slabbed(term, half // 2).astype(BF16)

    piece = cols // 4
    per_x = width // AX
    for c in range(3):
        for i in range(AX):
            mine = slice(i * per_x, (i + 1) * per_x)
            if c == 0:
                term = dot(feats_t[mine, 0:rows], dq_low)
            elif c == 1:
                term = dot(feats_t[mine, :], dk_low[...])
            else:
                term = dot(feats_t[mine, :], dv_low[...])
            term = term.reshape(AZ, AY, CAP, cols)
            for j in range(AY):
                strip = term[:, j].reshape(AZ * CAP, cols)
                first_ref[i, c, j] = slabbed(strip[:, : 2 * piece], piece).astype(BF16)
                second_ref[j, c, i] = slabbed(strip[:, 2 * piece :], piece).astype(BF16)


def layer(lists, valid, feats, table, weight, gain, grad):
    rows, width = feats.shape
    cols = grad.shape[1]
    keys = rows + table.shape[0]
    vmem = pl.BlockSpec(memory_space=pltpu.VMEM)
    smem = pl.BlockSpec(memory_space=pltpu.SMEM)
    strip = AZ * SLAB
    terms = N * SLAB + 2 * rows
    return pl.pallas_call(
        layer_kernel,
        out_shape=[
            jax.ShapeDtypeStruct((AX, 3, AY, strip, cols // 4), BF16),
            jax.ShapeDtypeStruct((AY, 3, AX, strip, cols // 4), BF16),
            jax.ShapeDtypeStruct((terms, width // 4), BF16),
            jax.ShapeDtypeStruct((terms, width // 4), BF16),
        ],
        in_specs=[smem, smem] + [vmem] * 5,
        out_specs=[vmem] * 4,
        scratch_shapes=[
            pltpu.VMEM((width, keys), BF16),
            pltpu.VMEM((keys, cols), BF16),
            pltpu.VMEM((cols, keys), BF16),
            pltpu.VMEM((keys, cols), F32),
            pltpu.VMEM((keys, cols), F32),
            pltpu.VMEM((keys, cols), BF16),
            pltpu.VMEM((rows, cols), F32),
            pltpu.VMEM((rows, cols), F32),
            pltpu.VMEM((cols, rows), F32),
            pltpu.VMEM((cols, rows), F32),
            pltpu.VMEM((keys, rows), F32),
            pltpu.VMEM((2, keys, rows), F32),
            pltpu.VMEM((2, keys, rows), F32),
            pltpu.VMEM((cols, rows), F32),
            pltpu.VMEM((keys, cols), F32),
            pltpu.VMEM((keys, cols), F32),
            pltpu.VMEM((keys, cols), BF16),
            pltpu.VMEM((keys, cols), BF16),
        ],
        compiler_params=pltpu.CompilerParams(vmem_limit_bytes=60 * 1024 * 1024),
        name="layer",
    )(lists, valid, feats, table, weight, gain, grad)


def axis_copies(src_of, landing, send_sems, recv_sems, axis_size, peer_of):
    copies = []
    for step in range(1, axis_size):
        copy = pltpu.make_async_remote_copy(
            src_ref=src_of(step),
            dst_ref=landing.at[step - 1],
            send_sem=send_sems.at[step - 1],
            recv_sem=recv_sems.at[step - 1],
            device_id={"dom": peer_of(step)},
            device_id_type=MESH,
        )
        copy.start()
        copies.append(copy)
    return copies


def reduce_kernel(
    idx_ref,
    first_ref,
    second_ref,
    keep_ref,
    send_ref,
    proj_ref,
    input_ref,
    pair_land,
    outgoing,
    landed,
    a_land,
    b_land,
    a_held,
    b_held,
    a_land2,
    b_land2,
    a_held2,
    b_held2,
    a_land3,
    b_land3,
    send_sem,
    recv_sem,
    pair_send,
    pair_recv,
    a_send,
    a_recv,
    b_send,
    b_recv,
    a_send2,
    a_recv2,
    b_send2,
    b_recv2,
    a_send3,
    a_recv3,
    b_send3,
    b_recv3,
):
    mine = place()
    dom, core, x, z, y = mine
    barrier = greet_all(dom, core)
    quarter = keep_ref.shape[1]
    own_rows = keep_ref.shape[0] - N * SLAB

    def at_x(step):
        return lax.rem(x + step, AX)

    def at_y(step):
        return lax.rem(y + step, AY)

    def at_z(step):
        return lax.rem(z + step, AZ)

    def peer_x(step):
        return at_x(step) * (AZ * AY) + z * AY + y

    def peer_y(step):
        return x * (AZ * AY) + z * AY + at_y(step)

    def peer_z(step):
        return x * (AZ * AY) + at_z(step) * AY + y

    pl.semaphore_wait(barrier, N)
    pairs = []
    for step in range(AX + 1):
        if step < AX:
            part = rows_at(at_x(step) * BLOCK, BLOCK)
        else:
            part = pl.ds(N * SLAB, own_rows)
        pair = pltpu.make_async_remote_copy(
            src_ref=send_ref.at[part],
            dst_ref=pair_land.at[part],
            send_sem=pair_send.at[step],
            recv_sem=pair_recv.at[step],
            device_id={"mp": 1 - core},
            device_id_type=MESH,
        )
        pair.start()
        pairs.append(pair)
    a_copies = axis_copies(lambda s: first_ref.at[at_x(s)], a_land, a_send, a_recv, AX, peer_x)
    b_copies = axis_copies(lambda s: second_ref.at[at_y(s)], b_land, b_send, b_recv, AY, peer_y)
    for step in range(AX):
        part = rows_at(at_x(step) * BLOCK, BLOCK)
        pairs[step].wait()
        outgoing[part, :] = (keep_ref[part, :].astype(F32) + pair_land[part, :].astype(F32)).astype(BF16)
        push_block(step, mine, outgoing, landed, send_sem, recv_sem)
    own = rows_at(dom * SLAB, SLAB)
    landed[own, :] = outgoing[own, :]

    def total(own_part, landing):
        result = own_part.astype(F32)
        for s in range(landing.shape[0]):
            result += landing[s].astype(F32)
        return result

    for copy in a_copies:
        copy.wait()
    a_held[...] = total(first_ref[x], a_land).astype(BF16)
    a_copies = axis_copies(lambda s: a_held.at[:, at_y(s)], a_land2, a_send2, a_recv2, AY, peer_y)
    for copy in b_copies:
        copy.wait()
    b_held[...] = total(second_ref[y], b_land).astype(BF16)
    b_copies = axis_copies(lambda s: b_held.at[:, at_x(s)], b_land2, b_send2, b_recv2, AX, peer_x)
    for copy in a_copies:
        copy.wait()
    a_held2[...] = total(a_held[:, y], a_land2).astype(BF16)
    a_copies = axis_copies(
        lambda s: a_held2.at[:, rows_at(at_z(s) * SLAB, SLAB)], a_land3, a_send3, a_recv3, AZ, peer_z
    )
    for copy in b_copies:
        copy.wait()
    b_held2[...] = total(b_held[:, x], b_land2).astype(BF16)
    b_copies = axis_copies(
        lambda s: b_held2.at[:, rows_at(at_z(s) * SLAB, SLAB)], b_land3, b_send3, b_recv3, AZ, peer_z
    )

    pairs[AX].wait()
    fixed = pl.ds(N * SLAB, own_rows)
    result = keep_ref[fixed, :].astype(F32) + pair_land[fixed, :].astype(F32)
    for step in range(AX):
        near = lax.rem(x - step + AX, AX)
        if step == 0:
            wait_bytes(landed.at[pl.ds(0, BLOCK - SLAB)], recv_sem.at[step])
        else:
            wait_bytes(landed.at[rows_at(near * BLOCK, BLOCK)], recv_sem.at[step])
        kinds = lax.broadcasted_iota(jnp.int32, (own_rows, BLOCK), 0)
        pick = jnp.where(kinds == idx_ref[near], 1.0, 0.0).astype(BF16)
        result += dot(pick, landed[rows_at(near * BLOCK, BLOCK), :])
    input_ref[:, 0:quarter] = result[: own_rows // 2].astype(BF16)
    input_ref[:, quarter:] = result[own_rows // 2 :].astype(BF16)

    piece = a_land3.shape[3]
    mine_z = rows_at(z * SLAB, SLAB)
    for copy in a_copies:
        copy.wait()
    done = total(a_held2[:, mine_z, :], a_land3)
    proj_ref[:, :, 0:piece] = done[:, :CAP]
    proj_ref[:, :, piece : 2 * piece] = done[:, CAP:]
    for copy in b_copies:
        copy.wait()
    done = total(b_held2[:, mine_z, :], b_land3)
    proj_ref[:, :, 2 * piece : 3 * piece] = done[:, :CAP]
    proj_ref[:, :, 3 * piece :] = done[:, CAP:]
    wait_bytes(outgoing.at[pl.ds(0, (N - 1) * SLAB)], send_sem)


def reduce_all(idx, first, second, keep, send):
    terms, quarter = keep.shape
    strip, piece = first.shape[3:]
    vmem = pl.BlockSpec(memory_space=pltpu.VMEM)
    dma = pltpu.SemaphoreType.DMA
    return pl.pallas_call(
        reduce_kernel,
        out_shape=[
            jax.ShapeDtypeStruct((3, CAP, 4 * piece), F32),
            jax.ShapeDtypeStruct(((terms - N * SLAB) // 2, 2 * quarter), BF16),
        ],
        in_specs=[vmem] * 5,
        out_specs=[vmem] * 2,
        scratch_shapes=[
            pltpu.VMEM((terms, quarter), BF16),
            pltpu.VMEM((N * SLAB, quarter), BF16),
            pltpu.VMEM((N * SLAB, quarter), BF16),
            pltpu.VMEM((AX - 1, 3, AY, strip, piece), BF16),
            pltpu.VMEM((AY - 1, 3, AX, strip, piece), BF16),
            pltpu.VMEM((3, AY, strip, piece), BF16),
            pltpu.VMEM((3, AX, strip, piece), BF16),
            pltpu.VMEM((AY - 1, 3, strip, piece), BF16),
            pltpu.VMEM((AX - 1, 3, strip, piece), BF16),
            pltpu.VMEM((3, strip, piece), BF16),
            pltpu.VMEM((3, strip, piece), BF16),
            pltpu.VMEM((AZ - 1, 3, SLAB, piece), BF16),
            pltpu.VMEM((AZ - 1, 3, SLAB, piece), BF16),
            dma,
            dma((AX,)),
            dma((AX + 1,)),
            dma((AX + 1,)),
            dma((AX - 1,)),
            dma((AX - 1,)),
            dma((AY - 1,)),
            dma((AY - 1,)),
            dma((AY - 1,)),
            dma((AY - 1,)),
            dma((AX - 1,)),
            dma((AX - 1,)),
            dma((AZ - 1,)),
            dma((AZ - 1,)),
            dma((AZ - 1,)),
            dma((AZ - 1,)),
        ],
        compiler_params=pltpu.CompilerParams(
            collective_id=1, has_side_effects=True, vmem_limit_bytes=40 * 1024 * 1024
        ),
        name="reduce_all",
    )(idx, first, second, keep, send)


def body(
    node_feats, proj_weight, norm_gain, grad_out, tile_lists, tile_valid, send_rows, send_count
):
    rows = node_feats.shape[0]
    live = jnp.arange(CAP, dtype=jnp.int32)[None, :] < send_count.reshape(N, 1)
    left = jnp.where(live, send_rows, 2 * rows)
    right = jnp.where(live, send_rows + rows, 2 * rows)
    idx = jnp.concatenate([left, right], axis=1).reshape(AX, 1, BLOCK)
    weight = jnp.transpose(proj_weight, (1, 0, 2))
    table = fetch(idx, node_feats)
    first, second, keep, send = layer(
        tile_lists, tile_valid, node_feats, table, weight, norm_gain, grad_out
    )
    proj_grad, input_grad = reduce_all(idx, first, second, keep, send)
    return (jnp.transpose(proj_grad, (1, 0, 2)), input_grad)


def solution(mesh):
    in_specs = (
        P("dom", None),
        P(None, None, "mp"),
        P(None, "mp"),
        P("dom", "mp"),
        P("dom", None),
        P("dom"),
        P("dom", None),
        P("dom", None),
    )
    out_specs = (P("dom", None, "mp"), P("dom", "mp"))
    return jax.shard_map(body, mesh=mesh, in_specs=in_specs, out_specs=out_specs, check_vma=False)
```

time: 1090 us -> 127 us (0.12); the launches traced: 1070 us -> 127 us
  waiting for transfers between devices: 757 us -> 0 us
  Pallas kernels: 0 us -> 116 us
  local copies, waits for them, and re-layouts: 117 us -> 9.34 us
  other arithmetic: 104 us -> 0.7 us
  starting transfers between devices: 36.5 us -> 0 us
  matrix products: 28.3 us -> 0 us
  between operations: 16.1 us -> 0.67 us
  loops' own time: 15 us -> 0 us
    reduce_scatter x1 -> x0, waiting for transfers between devices: 676 us -> none  [body(): lax.psum_scatter(grad_term, 'dom', scatter_dimension=0, tiled=True)]
    pallas_call x0 -> x3, Pallas kernels: none -> 116 us  [the longest x1 51.1 us: reduce_all(): pl.pallas_call(reduce_kernel, out_shape=[jax.ShapeDtypeStruct((3, CAP, 4...]
    scatter-add x6 -> x0, other arithmetic: 80 us -> none  [the longest x2 31.6 us: one_tile(): value_acc.at[listed].add(grad_values.reshape(list_len, flat_width))]
    all_to_all x3 -> x0, waiting for transfers between devices: 67.4 us -> none  [the longest x1 37.9 us: body(): lax.all_to_all(outgoing, 'dom', split_axis=0, concat_axis=0, tiled=True)]
    all_to_all x3 -> x0, starting transfers between devices: 36.4 us -> none  [the longest x1 15 us: body(): lax.all_to_all(send_count, 'dom', split_axis=1, concat_axis=0, tiled=True)]
    dot_general x15 -> x0, matrix products: 28.3 us -> none  [the longest x2 5.87 us: one_tile(): jnp.einsum('hqk,khd->qhd', prob_low, value_rows, preferred_element_type=j...]
    reshape x12 -> x1, local copies, waits for them, and re-layouts: 25.1 us -> 0.09 us  [body(): idx = jnp.concatenate([left, right], axis=1).reshape(AX, 1, BLOCK)]
    gather x12 -> x0, local copies, waits for them, and re-layouts: 22 us -> none  [the longest x2 10.1 us: body(): outgoing = jnp.concatenate([k_hat[flat_rows], values[flat_rows]], axis=1)]
  transfers between devices with their start and end apart: 5 -> 0, of which waited for: 4 -> 0; matrix products, arithmetic and copies ran while one was open for 7% -> 0% of each run, Pallas kernels for 0% -> 0%
where the time goes in v1:
time: 127 us
  Pallas kernels  116 us (91%)
  local copies, waits for them, and re-layouts  9.34 us (7%)
    pallas_call x1, Pallas kernels, reduce_all(): pl.pallas_call(reduce_kernel, out_shape=[jax.ShapeDtypeStruct((3, CAP, 4...  51.1 us
    pallas_call x1, Pallas kernels, fetch(): pl.pallas_call(fetch_kernel, out_shape=jax.ShapeDtypeStruct((N * CAP, wid...  38.1 us
    pallas_call x1, Pallas kernels, layer(): pl.pallas_call(layer_kernel, out_shape=[jax.ShapeDtypeStruct((AX, 3, AY,...  26.9 us
    unnamed x14, local copies, waits for them, and re-layouts  9.15 us

profile of v1, /device:TPU:32, one launch (start us, length us, event | category | flops | bytes accessed | tf_op | source)
XLA Modules:
  0.0 126.8 jit_solution(63609719385867993)
XLA Ops:
  0.6 0.7 fusion
  1.3 0.1 copy.11
  1.4 0.1 reshape.10.idx_ref
  1.5 0.0 copy-start.1
  1.5 1.0 copy-done.1
  2.6 38.1 %fetch.1.table_ref = bf16[1024,1024]{1,0:T(8,128)(2,1)S(1)} custom-call(s32[4,1,512]{2,1,0:T(1,128)S(1)} %reshape.10.idx_ref, bf16[256,1024]{1,0:T(8,128)(2,1)S(1)} %copy-done.1), custom_call_target="tpu_custom_call" | custom-call | tf_op jit(solution)/shard_map/fetch/pallas_call | solution.py:149
  40.7 0.0 copy-start
  40.7 1.3 %copy-done = bf16[1024,1024]{1,0:T(8,128)(2,1)} copy-done((bf16[1024,1024]{1,0:T(8,128)(2,1)}, bf16[1024,1024]{1,0:T(8,128)(2,1)S(1)}, u32[]{:S(2)}) %copy-start) | copy-done | bytes 2097176
  42.1 26.9 %layer.1 = (bf16[4,3,4,128,128]{4,3,2,1,0:T(8,128)(2,1)}, bf16[4,3,4,128,128]{4,3,2,1,0:T(8,128)(2,1)}, bf16[2560,256]{1,0:T(8,128)(2,1)}, bf16[2560,256]{1,0:T(8,128)(2,1)}) custom-call(s32[2,6]{1,0:T(2,128)} %lists_ref.1, s32[2]{0:T(128)} %valid_ref.1, bf16[256,1024]{1,0:T(8,128)(2,1)} %feats_ref.3, bf16[1024,1024]{1,0:T(8,128)(2,1)} %copy-done, ...), custom_call_target="tpu_custom_call" | custom-call | tf_op jit(solution)/shard_map/layer/pallas_call | solution.py:358
  69.0 0.0 copy-start.2
  69.0 1.4 %copy-done.2 = bf16[4,3,4,128,128]{4,3,2,1,0:T(8,128)(2,1)S(1)} copy-done((bf16[4,3,4,128,128]{4,3,2,1,0:T(8,128)(2,1)S(1)}, bf16[4,3,4,128,128]{4,3,2,1,0:T(8,128)(2,1)}, u32[]{:S(2)}) %copy-start.2) | copy-done | bytes 1572888
  70.4 0.0 copy-start.3
  70.4 1.4 %copy-done.3 = bf16[4,3,4,128,128]{4,3,2,1,0:T(8,128)(2,1)S(1)} copy-done((bf16[4,3,4,128,128]{4,3,2,1,0:T(8,128)(2,1)S(1)}, bf16[4,3,4,128,128]{4,3,2,1,0:T(8,128)(2,1)}, u32[]{:S(2)}) %copy-start.3) | copy-done | bytes 1572888
  71.8 0.0 copy-start.4
  71.8 1.3 %copy-done.4 = bf16[2560,256]{1,0:T(8,128)(2,1)S(1)} copy-done((bf16[2560,256]{1,0:T(8,128)(2,1)S(1)}, bf16[2560,256]{1,0:T(8,128)(2,1)}, u32[]{:S(2)}) %copy-start.4) | copy-done | bytes 1310744
  73.1 0.0 copy-start.5
  73.1 1.3 %copy-done.5 = bf16[2560,256]{1,0:T(8,128)(2,1)S(1)} copy-done((bf16[2560,256]{1,0:T(8,128)(2,1)S(1)}, bf16[2560,256]{1,0:T(8,128)(2,1)}, u32[]{:S(2)}) %copy-start.5) | copy-done | bytes 1310744
  74.4 51.1 %reduce_all.1 = (f32[3,8,512]{2,1,0:T(8,128)S(1)}, bf16[256,512]{1,0:T(8,128)(2,1)S(1)}) custom-call(s32[4,1,512]{2,1,0:T(1,128)S(1)} %reshape.10.idx_ref, bf16[4,3,4,128,128]{4,3,2,1,0:T(8,128)(2,1)S(1)} %copy-done.2, bf16[4,3,4,128,128]{4,3,2,1,0:T(8,128)(2,1)S(1)} %copy-done.3, bf16[2560,256]{1,0:T(8,128)(2,1)S(1)} %copy-done.4, ...), custom_call_target="tpu_custom_call" | custom-call | tf_op jit(solution)/shard_map/reduce_all/pallas_call | solution.py:560
  125.5 0.6 copy.16
  126.1 0.7 copy.17
  (1 shorter events, 0.0 us)
Async XLA Ops:
  1.5 1.0 copy-start.1
  40.7 1.3 %copy-start = (bf16[1024,1024]{1,0:T(8,128)(2,1)}, bf16[1024,1024]{1,0:T(8,128)(2,1)S(1)}, u32[]{:S(2)}) copy-start(bf16[1024,1024]{1,0:T(8,128)(2,1)S(1)} %fetch.1.table_ref) | copy-start | bytes 6291460
  69.0 1.4 %copy-start.2 = (bf16[4,3,4,128,128]{4,3,2,1,0:T(8,128)(2,1)S(1)}, bf16[4,3,4,128,128]{4,3,2,1,0:T(8,128)(2,1)}, u32[]{:S(2)}) copy-start(bf16[4,3,4,128,128]{4,3,2,1,0:T(8,128)(2,1)} %get-tuple-element.8.first_ref) | copy-start | bytes 4718596
  70.4 1.4 %copy-start.3 = (bf16[4,3,4,128,128]{4,3,2,1,0:T(8,128)(2,1)S(1)}, bf16[4,3,4,128,128]{4,3,2,1,0:T(8,128)(2,1)}, u32[]{:S(2)}) copy-start(bf16[4,3,4,128,128]{4,3,2,1,0:T(8,128)(2,1)} %get-tuple-element.9.second_ref) | copy-start | bytes 4718596
  71.8 1.3 %copy-start.4 = (bf16[2560,256]{1,0:T(8,128)(2,1)S(1)}, bf16[2560,256]{1,0:T(8,128)(2,1)}, u32[]{:S(2)}) copy-start(bf16[2560,256]{1,0:T(8,128)(2,1)} %get-tuple-element.10.keep_ref) | copy-start | bytes 3932164
  73.1 1.3 %copy-start.5 = (bf16[2560,256]{1,0:T(8,128)(2,1)S(1)}, bf16[2560,256]{1,0:T(8,128)(2,1)}, u32[]{:S(2)}) copy-start(bf16[2560,256]{1,0:T(8,128)(2,1)} %get-tuple-element.11.send_ref) | copy-start | bytes 3932164

commit v2 on v0

v2 whole, which is shorter than its diff:
```python
import math

import jax
import jax.numpy as jnp
from jax import lax
from jax.experimental import pallas as pl
from jax.experimental.pallas import tpu as pltpu
from jax.sharding import PartitionSpec as P

DH = 64
TILE = 128
CAP = 8
SLAB = 2 * CAP
EPS = 1e-06
AX, AZ, AY = 4, 8, 4
N = AX * AZ * AY
DEAD = 1024.0
LIVE_MAX = 512.0
LOG2E = math.log2(math.e)
MESH = pl.DeviceIdType.MESH
F32 = jnp.float32
BF16 = jnp.bfloat16


def dot(a, b):
    return jnp.dot(a, b, preferred_element_type=F32)


def dot_nt(a, b):
    return lax.dot_general(a, b, (((1,), (1,)), ((), ())), preferred_element_type=F32)


def dot_tn(a, b):
    return lax.dot_general(a, b, (((0,), (0,)), ((), ())), preferred_element_type=F32)


def place():
    dom = lax.axis_index("dom")
    core = lax.axis_index("mp")
    return dom, core, dom // (AZ * AY), lax.rem(dom // AY, AZ), lax.rem(dom, AY)


def rows_at(start, size):
    return pl.ds(pl.multiple_of(start, SLAB), size)


def greet_all(dom, core):
    barrier = pltpu.get_barrier_semaphore()

    def greet(i, carry):
        peer = lax.rem(dom + 1 + i, N)
        pl.semaphore_signal(barrier, inc=1, device_id={"dom": peer}, device_id_type=MESH)
        return carry

    lax.fori_loop(0, N - 1, greet, 0)
    pl.semaphore_signal(barrier, inc=1, device_id={"mp": 1 - core}, device_id_type=MESH)
    return barrier


def wait_bytes(ref, sem):
    pltpu.make_async_copy(ref, ref, sem).wait()


BLOCK = AZ * AY * SLAB
BLOCK_KEYS = AZ * AY * CAP


def push_block(step, mine, src, dst, send_sem, recv_sem):
    dom, core, x, z, y = mine
    far = lax.rem(x + step, AX)

    def push(i, carry):
        dz, dy = i // AY, lax.rem(i, AY)
        peer = far * (AZ * AY) + lax.rem(z + dz, AZ) * AY + lax.rem(y + dy, AY)
        pltpu.make_async_remote_copy(
            src_ref=src.at[rows_at(peer * SLAB, SLAB)],
            dst_ref=dst.at[rows_at(dom * SLAB, SLAB)],
            send_sem=send_sem,
            recv_sem=recv_sem.at[step],
            device_id={"dom": peer},
            device_id_type=MESH,
        ).start()
        return carry

    lax.fori_loop(1 if step == 0 else 0, AZ * AY, push, 0)


def wait_block(step, near, landed, recv_sem):
    if step == 0:
        wait_bytes(landed.at[pl.ds(0, BLOCK - SLAB)], recv_sem.at[step])
    else:
        wait_bytes(landed.at[rows_at(near * BLOCK, BLOCK)], recv_sem.at[step])


def to_other_core(src, dst, core, send_sem, recv_sem):
    copy = pltpu.make_async_remote_copy(
        src_ref=src,
        dst_ref=dst,
        send_sem=send_sem,
        recv_sem=recv_sem,
        device_id={"mp": 1 - core},
        device_id_type=MESH,
    )
    copy.start()
    return copy


def slabbed(block, width):
    count = block.shape[0] // CAP
    left = block[:, :width].reshape(count, CAP, width)
    right = block[:, width:].reshape(count, CAP, width)
    return jnp.concatenate([left, right], axis=1).reshape(count * SLAB, width)


def axis_copy(step, src, landing, send_sems, recv_sems, peer):
    copy = pltpu.make_async_remote_copy(
        src_ref=src,
        dst_ref=landing.at[step - 1],
        send_sem=send_sems.at[step - 1],
        recv_sem=recv_sems.at[step - 1],
        device_id={"dom": peer},
        device_id_type=MESH,
    )
    copy.start()
    return copy


def total_of(own_part, landing):
    result = own_part.astype(F32)
    for s in range(landing.shape[0]):
        result += landing[s].astype(F32)
    return result


def layer_kernel(
    lists_ref,
    valid_ref,
    idx_ref,
    feats_ref,
    weight_ref,
    gain_ref,
    grad_ref,
    proj_ref,
    input_ref,
    halves,
    outgoing,
    landed,
    feats_t,
    k_hat,
    k_hat_t,
    k_unit,
    k_inv,
    values,
    q_unit,
    q_inv,
    q_t,
    g_t,
    q_head,
    g_head,
    mask_t,
    expo,
    expo_dp,
    total,
    moment,
    dq_t,
    dk_sum,
    dk_low,
    dv_low,
    dq_low,
    keep,
    give,
    pair_land,
    back,
    back_land,
    first,
    second,
    a_land,
    b_land,
    a_held,
    b_held,
    a_land2,
    b_land2,
    a_held2,
    b_held2,
    a_land3,
    b_land3,
    send_sem,
    recv_sem,
    half_send,
    half_recv,
    pair_send,
    pair_recv,
    back_send,
    back_recv,
    a_send,
    a_recv,
    b_send,
    b_recv,
    a_send2,
    a_recv2,
    b_send2,
    b_recv2,
    a_send3,
    a_recv3,
    b_send3,
    b_recv3,
):
    mine = place()
    dom, core, x, z, y = mine
    barrier = greet_all(dom, core)
    rows, width = feats_ref.shape
    cols = grad_ref.shape[1]
    half = width // 2
    quarter = half // 2
    heads = cols // DH
    own_slab = rows_at(dom * SLAB, SLAB)
    own_tiles = rows // TILE

    def at_x(step):
        return lax.rem(x + step, AX)

    def at_y(step):
        return lax.rem(y + step, AY)

    def at_z(step):
        return lax.rem(z + step, AZ)

    def peer_x(step):
        return at_x(step) * (AZ * AY) + z * AY + y

    def peer_y(step):
        return x * (AZ * AY) + z * AY + at_y(step)

    def peer_z(step):
        return x * (AZ * AY) + at_z(step) * AY + y

    halves[0:rows, :] = feats_ref[:, pl.ds(pl.multiple_of(core * half, half), quarter)]
    halves[rows : 2 * rows, :] = feats_ref[
        :, pl.ds(pl.multiple_of(core * half + quarter, quarter), quarter)
    ]
    halves[2 * rows :, :] = jnp.full((SLAB, quarter), DEAD, BF16)
    for step in range(AX):
        far = at_x(step)
        kinds = lax.broadcasted_iota(jnp.int32, (2 * rows + SLAB, BLOCK), 0)
        pick = jnp.where(kinds == idx_ref[far], 1.0, 0.0).astype(BF16)
        outgoing[rows_at(far * BLOCK, BLOCK), :] = dot_tn(pick, halves[...]).astype(BF16)
        if step == 0:
            pl.semaphore_wait(barrier, N)
        push_block(step, mine, outgoing, landed.at[core], send_sem, recv_sem)
    landed[core, own_slab, :] = outgoing[own_slab, :]

    head_of = lax.broadcasted_iota(jnp.int32, (cols, cols), 0) // DH
    head_to = lax.broadcasted_iota(jnp.int32, (cols, cols), 1) // DH
    head_mean = jnp.where(head_of == head_to, 1.0 / DH, 0.0).astype(BF16)
    which = lax.broadcasted_iota(jnp.int32, (2 * DH, rows), 0) // DH

    def part_of(b):
        return pl.ds(b * rows, rows)

    def lanes_of(pair):
        return pl.ds(pl.multiple_of(pair * 2 * DH, 2 * DH), 2 * DH)

    def normed(mixed):
        inv = lax.rsqrt(dot((mixed * mixed).astype(BF16), head_mean) + EPS)
        return mixed * inv, inv

    def consume(b, block, tile_live, first_tile):
        part = part_of(b)
        feats_t[:, part] = block.T
        unit, inv = normed(dot(block, weight_ref[1]))
        k_inv[part, :] = inv
        k_unit[part, :] = unit
        low = (unit * gain_ref[1:2, :]).astype(BF16)
        k_hat[part, :] = low
        k_hat_t[:, part] = low.T
        values[part, :] = dot(block, weight_ref[2]).astype(BF16)
        for j in range(own_tiles):
            for t in range(own_tiles):
                listed = jnp.int32(0)
                for i in range(lists_ref.shape[1]):
                    listed += jnp.where(lists_ref[t, i] == first_tile + j, 1, 0)
                mask_t[j * TILE : (j + 1) * TILE, t * TILE : (t + 1) * TILE] = (
                    tile_live(j) * listed.astype(F32)
                )

        def head_pair(pair, carry):
            lanes = lanes_of(pair)
            k_pair = k_hat[part, lanes]
            v_pair = values[part, lanes]
            for h in range(2):
                head = pair * 2 + h
                low = (jnp.exp2(dot(k_pair, q_head[head])) * mask_t[...]).astype(BF16)
                expo[head, part, :] = low
                e = low.astype(F32)
                e_dp = e * dot(v_pair, g_head[head])
                expo_dp[head, part, :] = e_dp
                if b == 0:
                    total[head] = jnp.sum(e, axis=0, keepdims=True)
                    moment[head] = jnp.sum(e_dp, axis=0, keepdims=True)
                else:
                    total[head] += jnp.sum(e, axis=0, keepdims=True)
                    moment[head] += jnp.sum(e_dp, axis=0, keepdims=True)
            return carry

        lax.fori_loop(0, heads // 2, head_pair, 0)

    own_block = feats_ref[...]
    unit, inv = normed(dot(own_block, weight_ref[0]))
    q_inv[...] = inv
    q_unit[...] = unit
    q_t[...] = (unit * (gain_ref[0:1, :] * (LOG2E / math.sqrt(DH)))).T
    g_t[...] = grad_ref[...].astype(F32).T
    for head in range(heads):
        lanes = pl.ds(head // 2 * 2 * DH, 2 * DH)
        q_head[head] = jnp.where(which == head % 2, q_t[lanes, :], 0.0).astype(BF16)
        g_head[head] = jnp.where(which == head % 2, g_t[lanes, :], 0.0).astype(BF16)
    place_in_tile = lax.broadcasted_iota(jnp.int32, (TILE, TILE), 0)
    consume(0, own_block, lambda j: jnp.where(place_in_tile < valid_ref[j], 1.0, 0.0), 0)

    for step in range(AX):
        near = lax.rem(x - step + AX, AX)
        wait_block(step, near, landed.at[core], recv_sem)
        arrived = landed.at[core, rows_at(near * BLOCK, BLOCK)]
        pair = to_other_core(arrived, arrived, core, half_send.at[step], half_recv.at[step])
        pair.wait()
        strips = []
        for plane in range(2):
            slabs = landed[plane, rows_at(near * BLOCK, BLOCK), :].astype(F32)
            slabs = slabs.reshape(AZ * AY, SLAB, quarter)
            strips.append(slabs[:, :CAP, :].reshape(BLOCK_KEYS, quarter))
            strips.append(slabs[:, CAP:, :].reshape(BLOCK_KEYS, quarter))
        mark = strips[0][:, 0:1]

        def received_live(j):
            column = jnp.broadcast_to(mark[j * TILE : (j + 1) * TILE], (TILE, TILE))
            return jnp.where(column < LIVE_MAX, 1.0, 0.0)

        block = jnp.concatenate([strip.astype(BF16) for strip in strips], axis=1)
        consume(step + 1, block, received_live, own_tiles + near * own_tiles)

    for head in range(heads):
        lanes = pl.ds(head // 2 * 2 * DH, 2 * DH)
        over = 1.0 / total[head]
        moment[head] = moment[head] * over
        total[head] = over
        q_head[head] = jnp.where(
            which == head % 2, q_t[lanes, :] * (over * (1.0 / LOG2E)), 0.0
        ).astype(BF16)
        g_head[head] = jnp.where(which == head % 2, g_t[lanes, :] * over, 0.0).astype(BF16)

    def norm_back(unit, inv, upstream):
        inner = dot((unit * upstream).astype(BF16), head_mean)
        return inv * (upstream - unit * inner)

    pairs = []
    fixed = pl.ds(N * SLAB, 2 * rows)

    def finish(step):
        near = lax.rem(x - step + AX, AX)
        part = rows_at(near * BLOCK, BLOCK)
        local = pl.ds(step * BLOCK, BLOCK)
        pairs[step].wait()
        back[part, :] = (keep[local, :] + pair_land[local, :].astype(F32)).astype(BF16)
        push_block((AX - step) % AX, mine, back, back_land, back_send, back_recv)

    for step in range(AX + 1):
        b = (step + 1) % (AX + 1)
        part = part_of(b)

        def head_pair(pair, carry):
            lanes = lanes_of(pair)
            lows, slopes = [], []
            for h in range(2):
                head = pair * 2 + h
                low = expo[head, part, :]
                ds = (expo_dp[head, part, :] - low.astype(F32) * moment[head]).astype(BF16)
                head_rows = pl.ds(pl.multiple_of(head * DH, DH), DH)
                dq = dot(k_hat_t[head_rows, part], ds)
                if step == 0:
                    dq_t[head_rows, :] = dq
                else:
                    dq_t[head_rows, :] += dq
                lows.append(low)
                slopes.append(ds)
            g_both = jnp.concatenate([g_head[pair * 2], g_head[pair * 2 + 1]], axis=1)
            q_both = jnp.concatenate([q_head[pair * 2], q_head[pair * 2 + 1]], axis=1)
            dv_low[part, lanes] = dot_nt(jnp.concatenate(lows, axis=1), g_both).astype(BF16)
            dk_sum[:, lanes] = dot_nt(jnp.concatenate(slopes, axis=1), q_both)
            return carry

        lax.fori_loop(0, heads // 2, head_pair, 0)
        upstream = dk_sum[...] * gain_ref[1:2, :]
        dk_low[part, :] = norm_back(k_unit[part, :], k_inv[part, :], upstream).astype(BF16)
        if b == 0:
            for head in range(heads):
                head_rows = slice(head * DH, (head + 1) * DH)
                dq_t[head_rows, :] = dq_t[head_rows, :] * (total[head] * (1.0 / math.sqrt(DH)))
            upstream = dq_t[...].T * gain_ref[0:1, :]
            dq_low[...] = norm_back(q_unit[...], q_inv[...], upstream).astype(BF16)
        local = pl.ds(step * BLOCK, BLOCK)
        for side in range(2):
            near = core if side else 1 - core
            wanted = pl.ds(pl.multiple_of(near * half, half), half)
            term = dot_nt(dk_low[part, :], weight_ref[1, wanted, :])
            term += dot_nt(dv_low[part, :], weight_ref[2, wanted, :])
            if b == 0:
                term += dot_nt(dq_low[...], weight_ref[0, wanted, :])
                term = jnp.concatenate([term[:, :quarter], term[:, quarter:]], axis=0)
            else:
                term = slabbed(term, quarter)
            if side:
                keep[local, :] = term
            else:
                give[local, :] = term.astype(BF16)
                pairs.append(
                    to_other_core(
                        give.at[local],
                        pair_land.at[local],
                        core,
                        pair_send.at[step],
                        pair_recv.at[step],
                    )
                )
        if step > 0:
            finish(step - 1)
    back_land[own_slab, :] = back[own_slab, :]

    piece = cols // 4
    per_x = width // AX
    a_copies = []
    for step in (1, 2, 3, 0):
        i = at_x(step)
        chunk = pl.ds(pl.multiple_of(i * per_x, per_x), per_x)
        for c in range(3):
            if c == 0:
                term = dot(feats_t[chunk, 0:rows], dq_low[...])
            elif c == 1:
                term = dot(feats_t[chunk, :], dk_low[...])
            else:
                term = dot(feats_t[chunk, :], dv_low[...])
            term = term.reshape(AZ, AY, CAP, cols)
            for j in range(AY):
                strip = term[:, j].reshape(AZ * CAP, cols)
                first[i, c, j] = slabbed(strip[:, : 2 * piece], piece).astype(BF16)
                second[j, c, i] = slabbed(strip[:, 2 * piece :], piece).astype(BF16)
        if step > 0:
            a_copies.append(axis_copy(step, first.at[i], a_land, a_send, a_recv, peer_x(step)))
    b_copies = [
        axis_copy(s, second.at[at_y(s)], b_land, b_send, b_recv, peer_y(s)) for s in range(1, AY)
    ]

    for copy in a_copies:
        copy.wait()
    a_held[...] = total_of(first[x], a_land).astype(BF16)
    a_copies = [
        axis_copy(s, a_held.at[:, at_y(s)], a_land2, a_send2, a_recv2, peer_y(s))
        for s in range(1, AY)
    ]
    for copy in b_copies:
        copy.wait()
    b_held[...] = total_of(second[y], b_land).astype(BF16)
    b_copies = [
        axis_copy(s, b_held.at[:, at_x(s)], b_land2, b_send2, b_recv2, peer_x(s))
        for s in range(1, AX)
    ]
    for copy in a_copies:
        copy.wait()
    a_held2[...] = total_of(a_held[:, y], a_land2).astype(BF16)
    a_copies = [
        axis_copy(s, a_held2.at[:, rows_at(at_z(s) * SLAB, SLAB)], a_land3, a_send3, a_recv3, peer_z(s))
        for s in range(1, AZ)
    ]
    for copy in b_copies:
        copy.wait()
    b_held2[...] = total_of(b_held[:, x], b_land2).astype(BF16)
    b_copies = [
        axis_copy(s, b_held2.at[:, rows_at(at_z(s) * SLAB, SLAB)], b_land3, b_send3, b_recv3, peer_z(s))
        for s in range(1, AZ)
    ]

    pairs[AX].wait()
    local = pl.ds(AX * BLOCK, 2 * rows)
    result = keep[local, :] + pair_land[local, :].astype(F32)
    for step in (0, 3, 2, 1):
        near = lax.rem(x - step + AX, AX)
        wait_block(step, near, back_land, back_recv)
        kinds = lax.broadcasted_iota(jnp.int32, (2 * rows, BLOCK), 0)
        pick = jnp.where(kinds == idx_ref[near], 1.0, 0.0).astype(BF16)
        result += dot(pick, back_land[rows_at(near * BLOCK, BLOCK), :])
    input_ref[:, 0:quarter] = result[:rows].astype(BF16)
    input_ref[:, quarter:] = result[rows:].astype(BF16)

    mine_z = rows_at(z * SLAB, SLAB)
    for copy in a_copies:
        copy.wait()
    done = total_of(a_held2[:, mine_z, :], a_land3)
    proj_ref[:, :, 0:piece] = done[:, :CAP]
    proj_ref[:, :, piece : 2 * piece] = done[:, CAP:]
    for copy in b_copies:
        copy.wait()
    done = total_of(b_held2[:, mine_z, :], b_land3)
    proj_ref[:, :, 2 * piece : 3 * piece] = done[:, :CAP]
    proj_ref[:, :, 3 * piece :] = done[:, CAP:]
    wait_bytes(outgoing.at[pl.ds(0, (N - 1) * SLAB)], send_sem)
    wait_bytes(back.at[pl.ds(0, (N - 1) * SLAB)], back_send)


def layer(lists, valid, idx, feats, weight, gain, grad):
    rows, width = feats.shape
    cols = grad.shape[1]
    heads = cols // DH
    keys = rows + N * CAP
    quarter = width // 4
    piece = cols // 4
    strip = AZ * SLAB
    terms = N * SLAB + 2 * rows
    smem = pl.BlockSpec(memory_space=pltpu.SMEM)
    vmem = pl.BlockSpec(memory_space=pltpu.VMEM)
    ram = pltpu.VMEM
    dma = pltpu.SemaphoreType.DMA
    return pl.pallas_call(
        layer_kernel,
        out_shape=[
            jax.ShapeDtypeStruct((3, CAP, cols), F32),
            jax.ShapeDtypeStruct((rows, half_of(width)), BF16),
        ],
        in_specs=[smem, smem] + [vmem] * 5,
        out_specs=[vmem] * 2,
        scratch_shapes=[
            ram((2 * rows + SLAB, quarter), BF16),
            ram((N * SLAB, quarter), BF16),
            ram((2, N * SLAB, quarter), BF16),
            ram((width, keys), BF16),
            ram((keys, cols), BF16),
            ram((cols, keys), BF16),
            ram((keys, cols), F32),
            ram((keys, cols), F32),
            ram((keys, cols), BF16),
            ram((rows, cols), F32),
            ram((rows, cols), F32),
            ram((cols, rows), F32),
            ram((cols, rows), F32),
            ram((heads, 2 * DH, rows), BF16),
            ram((heads, 2 * DH, rows), BF16),
            ram((rows, rows), F32),
            ram((heads, keys, rows), BF16),
            ram((heads, keys, rows), F32),
            ram((heads, 1, rows), F32),
            ram((heads, 1, rows), F32),
            ram((cols, rows), F32),
            ram((rows, cols), F32),
            ram((keys, cols), BF16),
            ram((keys, cols), BF16),
            ram((rows, cols), BF16),
            ram((terms, quarter), F32),
            ram((terms, quarter), BF16),
            ram((terms, quarter), BF16),
            ram((N * SLAB, quarter), BF16),
            ram((N * SLAB, quarter), BF16),
            ram((AX, 3, AY, strip, piece), BF16),
            ram((AY, 3, AX, strip, piece), BF16),
            ram((AX - 1, 3, AY, strip, piece), BF16),
            ram((AY - 1, 3, AX, strip, piece), BF16),
            ram((3, AY, strip, piece), BF16),
            ram((3, AX, strip, piece), BF16),
            ram((AY - 1, 3, strip, piece), BF16),
            ram((AX - 1, 3, strip, piece), BF16),
            ram((3, strip, piece), BF16),
            ram((3, strip, piece), BF16),
            ram((AZ - 1, 3, SLAB, piece), BF16),
            ram((AZ - 1, 3, SLAB, piece), BF16),
            dma,
            dma((AX,)),
            dma((AX,)),
            dma((AX,)),
            dma((AX + 1,)),
            dma((AX + 1,)),
            dma,
            dma((AX,)),
            dma((AX - 1,)),
            dma((AX - 1,)),
            dma((AY - 1,)),
            dma((AY - 1,)),
            dma((AY - 1,)),
            dma((AY - 1,)),
            dma((AX - 1,)),
            dma((AX - 1,)),
            dma((AZ - 1,)),
            dma((AZ - 1,)),
            dma((AZ - 1,)),
            dma((AZ - 1,)),
        ],
        compiler_params=pltpu.CompilerParams(
            collective_id=0, has_side_effects=True, vmem_limit_bytes=60 * 1024 * 1024
        ),
        name="layer",
    )(lists, valid, idx, feats, weight, gain, grad)


def half_of(size):
    return size // 2


def body(
    node_feats, proj_weight, norm_gain, grad_out, tile_lists, tile_valid, send_rows, send_count
):
    rows = node_feats.shape[0]
    live = jnp.arange(CAP, dtype=jnp.int32)[None, :] < send_count.reshape(N, 1)
    left = jnp.where(live, send_rows, 2 * rows)
    right = jnp.where(live, send_rows + rows, 2 * rows)
    idx = jnp.concatenate([left, right], axis=1).reshape(AX, 1, BLOCK)
    weight = jnp.transpose(proj_weight, (1, 0, 2))
    proj_grad, input_grad = layer(
        tile_lists, tile_valid, idx, node_feats, weight, norm_gain, grad_out
    )
    return (jnp.transpose(proj_grad, (1, 0, 2)), input_grad)


def solution(mesh):
    in_specs = (
        P("dom", None),
        P(None, None, "mp"),
        P(None, "mp"),
        P("dom", "mp"),
        P("dom", None),
        P("dom"),
        P("dom", None),
        P("dom", None),
    )
    out_specs = (P("dom", None, "mp"), P("dom", "mp"))
    return jax.shard_map(body, mesh=mesh, in_specs=in_specs, out_specs=out_specs, check_vma=False)
```

time: 1090 us -> 112 us (0.10); the launches traced: 1070 us -> 112 us
  waiting for transfers between devices: 757 us -> 0 us
  local copies, waits for them, and re-layouts: 117 us -> 3.89 us
  Pallas kernels: 0 us -> 107 us
  other arithmetic: 104 us -> 0.7 us
  starting transfers between devices: 36.5 us -> 0 us
  matrix products: 28.3 us -> 0 us
  between operations: 16.1 us -> 0.64 us
  loops' own time: 15 us -> 0 us
    reduce_scatter x1 -> x0, waiting for transfers between devices: 676 us -> none  [body(): lax.psum_scatter(grad_term, 'dom', scatter_dimension=0, tiled=True)]
    pallas_call x0 -> x1, Pallas kernels: none -> 107 us  [layer(): pl.pallas_call(layer_kernel, out_shape=[jax.ShapeDtypeStruct((3, CAP, col...]
    scatter-add x6 -> x0, other arithmetic: 80 us -> none  [the longest x2 31.6 us: one_tile(): value_acc.at[listed].add(grad_values.reshape(list_len, flat_width))]
    all_to_all x3 -> x0, waiting for transfers between devices: 67.4 us -> none  [the longest x1 37.9 us: body(): lax.all_to_all(outgoing, 'dom', split_axis=0, concat_axis=0, tiled=True)]
    all_to_all x3 -> x0, starting transfers between devices: 36.4 us -> none  [the longest x1 15 us: body(): lax.all_to_all(send_count, 'dom', split_axis=1, concat_axis=0, tiled=True)]
    dot_general x15 -> x0, matrix products: 28.3 us -> none  [the longest x2 5.87 us: one_tile(): jnp.einsum('hqk,khd->qhd', prob_low, value_rows, preferred_element_type=j...]
    reshape x12 -> x1, local copies, waits for them, and re-layouts: 25.1 us -> 0.69 us  [body(): idx = jnp.concatenate([left, right], axis=1).reshape(AX, 1, BLOCK)]
    gather x12 -> x0, local copies, waits for them, and re-layouts: 22 us -> none  [the longest x2 10.1 us: body(): outgoing = jnp.concatenate([k_hat[flat_rows], values[flat_rows]], axis=1)]
  transfers between devices with their start and end apart: 5 -> 0, of which waited for: 4 -> 0; matrix products, arithmetic and copies ran while one was open for 7% -> 0% of each run, Pallas kernels for 0% -> 0%
where the time goes in v2:
time: 112 us
  Pallas kernels  107 us (96%)
  local copies, waits for them, and re-layouts  3.89 us (3%)
    pallas_call x1, Pallas kernels, layer(): pl.pallas_call(layer_kernel, out_shape=[jax.ShapeDtypeStruct((3, CAP, col...  107 us
    unnamed x2, local copies, waits for them, and re-layouts  3.09 us

profile of v2, /device:TPU:32, one launch (start us, length us, event | category | flops | bytes accessed | tf_op | source)
XLA Modules:
  0.0 111.8 jit_solution(4319558207071809177)
XLA Ops:
  0.6 0.7 fusion
  1.3 0.1 copy.11
  1.4 0.7 reshape.10.idx_ref
  2.1 106.6 %layer.1 = (f32[3,8,512]{2,1,0:T(8,128)}, bf16[256,512]{1,0:T(8,128)(2,1)}) custom-call(s32[2,6]{1,0:T(2,128)} %lists_ref.1, s32[2]{0:T(128)} %valid_ref.1, s32[4,1,512]{2,1,0:T(1,128)} %reshape.10.idx_ref, bf16[256,1024]{1,0:T(8,128)(2,1)} %feats_ref.1, bf16[3,1024,512]{2,1,0:T(8,128)(2,1)} %bitcast.3, f32[2,512]{1,0:T(2,128)} %gain_ref.1, ...), custom_call_target="tpu_custom_call" | custom-call | tf_op jit(solution)/shard_map/layer/pallas_call | solution.py:521
  108.7 1.4 %copy.15 = f32[8,3,512]{2,0,1:T(8,128)} copy(f32[8,3,512]{2,0,1:T(8,128)} %bitcast.4) | data formatting | bytes 98304
  110.1 1.7 %copy.16 = bf16[256,512]{1,0:T(8,128)(2,1)} copy(bf16[256,512]{1,0:T(8,128)(2,1)} %get-tuple-element.11) | data formatting | bytes 524288
  (1 shorter events, 0.0 us)

commit v3 on v2

--- a/solution.py
+++ b/solution.py
@@ -163,9 +163,7 @@
     total,
     moment,
     dq_t,
-    dk_sum,
-    dk_low,
-    dv_low,
+    kv_low,
     dq_low,
     keep,
     give,
@@ -347,140 +345,191 @@
             which == head % 2, q_t[lanes, :] * (over * (1.0 / LOG2E)), 0.0
         ).astype(BF16)
         g_head[head] = jnp.where(which == head % 2, g_t[lanes, :] * over, 0.0).astype(BF16)
+    dq_t[...] = jnp.zeros(dq_t.shape, F32)
+
+    pair_mean = head_mean[: 2 * DH, : 2 * DH]
 
     def norm_back(unit, inv, upstream):
-        inner = dot((unit * upstream).astype(BF16), head_mean)
+        inner = dot((unit * upstream).astype(BF16), pair_mean)
         return inv * (upstream - unit * inner)
 
+    def second_pass(pair):
+        lanes = slice(pair * 2 * DH, (pair + 1) * 2 * DH)
+        q_both = jnp.concatenate([q_head[pair * 2], q_head[pair * 2 + 1]], axis=1)
+        g_both = jnp.concatenate([g_head[pair * 2], g_head[pair * 2 + 1]], axis=1)
+
+        def key_block(b, carry):
+            part = pl.ds(pl.multiple_of(b * rows, rows), rows)
+            lows, slopes = [], []
+            for head in (pair * 2, pair * 2 + 1):
+                low = expo[head, part, :]
+                ds = (expo_dp[head, part, :] - low.astype(F32) * moment[head]).astype(BF16)
+                head_rows = slice(head * DH, (head + 1) * DH)
+                dq_t[head_rows, :] += dot(k_hat_t[head_rows, part], ds)
+                lows.append(low)
+                slopes.append(ds)
+            dv = dot_nt(jnp.concatenate(lows, axis=1), g_both)
+            dk = dot_nt(jnp.concatenate(slopes, axis=1), q_both) * gain_ref[1:2, lanes]
+            dk = norm_back(k_unit[part, lanes], k_inv[part, lanes], dk)
+            kv_low[pair, part, 0 : 2 * DH] = dk.astype(BF16)
+            kv_low[pair, part, 2 * DH :] = dv.astype(BF16)
+            return carry
+
+        lax.fori_loop(0, AX + 1, key_block, 0)
+        for head in (pair * 2, pair * 2 + 1):
+            head_rows = slice(head * DH, (head + 1) * DH)
+            dq_t[head_rows, :] = dq_t[head_rows, :] * (total[head] * (1.0 / math.sqrt(DH)))
+        upstream = dq_t[lanes, :].T * gain_ref[0:1, lanes]
+        dq_low[:, lanes] = norm_back(q_unit[:, lanes], q_inv[:, lanes], upstream).astype(BF16)
+
+    per_x = width // AX
+    strip = AZ * CAP
+
+    def gradient_columns(pair):
+        lanes = slice(pair * 2 * DH, (pair + 1) * 2 * DH)
+        turn = pair // 2
+        for i in range(AX):
+            chunk = slice(i * per_x, (i + 1) * per_x)
+            both = dot(feats_t[chunk, :], kv_low[pair])
+            terms = (
+                dot(feats_t[chunk, 0:rows], dq_low[:, lanes]),
+                both[:, : 2 * DH],
+                both[:, 2 * DH :],
+            )
+            for c in range(3):
+                term = terms[c].reshape(AZ, AY, CAP, 2 * DH)
+                for j in range(AY):
+                    tile = term[:, j].reshape(strip, 2 * DH).astype(BF16)
+                    if pair % 2 == 0:
+                        first[turn, i, c, j] = tile
+                    else:
+                        second[turn, j, c, i] = tile
+        if pair % 2 == 0:
+            return [
+                axis_copy(
+                    s,
+                    first.at[turn, at_x(s)],
+                    a_land.at[turn],
+                    a_send.at[turn],
+                    a_recv.at[turn],
+                    peer_x(s),
+                )
+                for s in range(1, AX)
+            ]
+        return [
+            axis_copy(
+                s,
+                second.at[turn, at_y(s)],
+                b_land.at[turn],
+                b_send.at[turn],
+                b_recv.at[turn],
+                peer_y(s),
+            )
+            for s in range(1, AY)
+        ]
+
+    second_pass(0)
+    a_first = gradient_columns(0)
+    second_pass(1)
+    b_first = gradient_columns(1)
+    second_pass(2)
+    second_pass(3)
+
     pairs = []
-    fixed = pl.ds(N * SLAB, 2 * rows)
-
-    def finish(step):
+
+    def term_of(step, near):
+        part = part_of((step + 1) % (AX + 1))
+        wanted = pl.ds(pl.multiple_of(near * half, half), half)
+        dk = jnp.concatenate([kv_low[p, part, 0 : 2 * DH] for p in range(heads // 2)], axis=1)
+        dv = jnp.concatenate([kv_low[p, part, 2 * DH :] for p in range(heads // 2)], axis=1)
+        term = dot_nt(dk, weight_ref[1, wanted, :]) + dot_nt(dv, weight_ref[2, wanted, :])
+        if step == AX:
+            term += dot_nt(dq_low[...], weight_ref[0, wanted, :])
+            return jnp.concatenate([term[:, :quarter], term[:, quarter:]], axis=0)
+        return slabbed(term, quarter)
+
+    def give_term(step):
+        local = pl.ds(step * BLOCK, BLOCK)
+        give[local, :] = term_of(step, 1 - core).astype(BF16)
+        pairs.append(
+            to_other_core(
+                give.at[local], pair_land.at[local], core, pair_send.at[step], pair_recv.at[step]
+            )
+        )
+
+    def return_term(step):
         near = lax.rem(x - step + AX, AX)
         part = rows_at(near * BLOCK, BLOCK)
         local = pl.ds(step * BLOCK, BLOCK)
+        kept = term_of(step, core)
         pairs[step].wait()
-        back[part, :] = (keep[local, :] + pair_land[local, :].astype(F32)).astype(BF16)
+        back[part, :] = (kept + pair_land[local, :].astype(F32)).astype(BF16)
         push_block((AX - step) % AX, mine, back, back_land, back_send, back_recv)
 
-    for step in range(AX + 1):
-        b = (step + 1) % (AX + 1)
-        part = part_of(b)
-
-        def head_pair(pair, carry):
-            lanes = lanes_of(pair)
-            lows, slopes = [], []
-            for h in range(2):
-                head = pair * 2 + h
-                low = expo[head, part, :]
-                ds = (expo_dp[head, part, :] - low.astype(F32) * moment[head]).astype(BF16)
-                head_rows = pl.ds(pl.multiple_of(head * DH, DH), DH)
-                dq = dot(k_hat_t[head_rows, part], ds)
-                if step == 0:
-                    dq_t[head_rows, :] = dq
-                else:
-                    dq_t[head_rows, :] += dq
-                lows.append(low)
-                slopes.append(ds)
-            g_both = jnp.concatenate([g_head[pair * 2], g_head[pair * 2 + 1]], axis=1)
-            q_both = jnp.concatenate([q_head[pair * 2], q_head[pair * 2 + 1]], axis=1)
-            dv_low[part, lanes] = dot_nt(jnp.concatenate(lows, axis=1), g_both).astype(BF16)
-            dk_sum[:, lanes] = dot_nt(jnp.concatenate(slopes, axis=1), q_both)
-            return carry
-
-        lax.fori_loop(0, heads // 2, head_pair, 0)
-        upstream = dk_sum[...] * gain_ref[1:2, :]
-        dk_low[part, :] = norm_back(k_unit[part, :], k_inv[part, :], upstream).astype(BF16)
-        if b == 0:
-            for head in range(heads):
-                head_rows = slice(head * DH, (head + 1) * DH)
-                dq_t[head_rows, :] = dq_t[head_rows, :] * (total[head] * (1.0 / math.sqrt(DH)))
-            upstream = dq_t[...].T * gain_ref[0:1, :]
-            dq_low[...] = norm_back(q_unit[...], q_inv[...], upstream).astype(BF16)
-        local = pl.ds(step * BLOCK, BLOCK)
-        for side in range(2):
-            near = core if side else 1 - core
-            wanted = pl.ds(pl.multiple_of(near * half, half), half)
-            term = dot_nt(dk_low[part, :], weight_ref[1, wanted, :])
-            term += dot_nt(dv_low[part, :], weight_ref[2, wanted, :])
-            if b == 0:
-                term += dot_nt(dq_low[...], weight_ref[0, wanted, :])
-                term = jnp.concatenate([term[:, :quarter], term[:, quarter:]], axis=0)
-            else:
-                term = slabbed(term, quarter)
-            if side:
-                keep[local, :] = term
-            else:
-                give[local, :] = term.astype(BF16)
-                pairs.append(
-                    to_other_core(
-                        give.at[local],
-                        pair_land.at[local],
-                        core,
-                        pair_send.at[step],
-                        pair_recv.at[step],
-                    )
-                )
-        if step > 0:
-            finish(step - 1)
+    give_term(0)
+    for step in range(AX):
+        give_term(step + 1)
+        return_term(step)
     back_land[own_slab, :] = back[own_slab, :]
-
-    piece = cols // 4
-    per_x = width // AX
-    a_copies = []
-    for step in (1, 2, 3, 0):
-        i = at_x(step)
-        chunk = pl.ds(pl.multiple_of(i * per_x, per_x), per_x)
-        for c in range(3):
-            if c == 0:
-                term = dot(feats_t[chunk, 0:rows], dq_low[...])
-            elif c == 1:
-                term = dot(feats_t[chunk, :], dk_low[...])
-            else:
-                term = dot(feats_t[chunk, :], dv_low[...])
-            term = term.reshape(AZ, AY, CAP, cols)
-            for j in range(AY):
-                strip = term[:, j].reshape(AZ * CAP, cols)
-                first[i, c, j] = slabbed(strip[:, : 2 * piece], piece).astype(BF16)
-                second[j, c, i] = slabbed(strip[:, 2 * piece :], piece).astype(BF16)
-        if step > 0:
-            a_copies.append(axis_copy(step, first.at[i], a_land, a_send, a_recv, peer_x(step)))
-    b_copies = [
-        axis_copy(s, second.at[at_y(s)], b_land, b_send, b_recv, peer_y(s)) for s in range(1, AY)
-    ]
-
-    for copy in a_copies:
+    a_second = gradient_columns(2)
+    b_second = gradient_columns(3)
+    keep[...] = term_of(AX, core)
+
+    def cross_a(turn, copies):
+        for copy in copies:
+            copy.wait()
+        a_held[turn] = total_of(first[turn, x], a_land.at[turn]).astype(BF16)
+        return [
+            axis_copy(
+                s,
+                a_held.at[turn, :, at_y(s)],
+                a_land2.at[turn],
+                a_send2.at[turn],
+                a_recv2.at[turn],
+                peer_y(s),
+            )
+            for s in range(1, AY)
+        ]
+
+    def cross_b(turn, copies):
+        for copy in copies:
+            copy.wait()
+        b_held[turn] = total_of(second[turn, y], b_land.at[turn]).astype(BF16)
+        return [
+            axis_copy(
+                s,
+                b_held.at[turn, :, at_x(s)],
+                b_land2.at[turn],
+                b_send2.at[turn],
+                b_recv2.at[turn],
+                peer_x(s),
+            )
+            for s in range(1, AX)
+        ]
+
+    def along_z(sums, held2, landing, send_sems, recv_sems):
+        sums = [part.reshape(3, AZ, CAP, 2 * DH) for part in sums]
+        held2[...] = jnp.concatenate(sums, axis=2).astype(BF16)
+        return [
+            axis_copy(s, held2.at[:, at_z(s)], landing, send_sems, recv_sems, peer_z(s))
+            for s in range(1, AZ)
+        ]
+
+    a_first = cross_a(0, a_first)
+    b_first = cross_b(0, b_first)
+    a_second = cross_a(1, a_second)
+    b_second = cross_b(1, b_second)
+    for copy in a_first + a_second:
         copy.wait()
-    a_held[...] = total_of(first[x], a_land).astype(BF16)
-    a_copies = [
-        axis_copy(s, a_held.at[:, at_y(s)], a_land2, a_send2, a_recv2, peer_y(s))
-        for s in range(1, AY)
-    ]
-    for copy in b_copies:
+    sums = [total_of(a_held[turn, :, y], a_land2.at[turn]) for turn in range(2)]
+    a_copies = along_z(sums, a_held2, a_land3, a_send3, a_recv3)
+    for copy in b_first + b_second:
         copy.wait()
-    b_held[...] = total_of(second[y], b_land).astype(BF16)
-    b_copies = [
-        axis_copy(s, b_held.at[:, at_x(s)], b_land2, b_send2, b_recv2, peer_x(s))
-        for s in range(1, AX)
-    ]
-    for copy in a_copies:
-        copy.wait()
-    a_held2[...] = total_of(a_held[:, y], a_land2).astype(BF16)
-    a_copies = [
-        axis_copy(s, a_held2.at[:, rows_at(at_z(s) * SLAB, SLAB)], a_land3, a_send3, a_recv3, peer_z(s))
-        for s in range(1, AZ)
-    ]
-    for copy in b_copies:
-        copy.wait()
-    b_held2[...] = total_of(b_held[:, x], b_land2).astype(BF16)
-    b_copies = [
-        axis_copy(s, b_held2.at[:, rows_at(at_z(s) * SLAB, SLAB)], b_land3, b_send3, b_recv3, peer_z(s))
-        for s in range(1, AZ)
-    ]
+    sums = [total_of(b_held[turn, :, x], b_land2.at[turn]) for turn in range(2)]
+    b_copies = along_z(sums, b_held2, b_land3, b_send3, b_recv3)
 
     pairs[AX].wait()
-    local = pl.ds(AX * BLOCK, 2 * rows)
-    result = keep[local, :] + pair_land[local, :].astype(F32)
+    result = keep[...] + pair_land[pl.ds(AX * BLOCK, 2 * rows), :].astype(F32)
     for step in (0, 3, 2, 1):
         near = lax.rem(x - step + AX, AX)
         wait_block(step, near, back_land, back_recv)
@@ -490,20 +539,17 @@
     input_ref[:, 0:quarter] = result[:rows].astype(BF16)
     input_ref[:, quarter:] = result[rows:].astype(BF16)
 
-    mine_z = rows_at(z * SLAB, SLAB)
-    for copy in a_copies:
-        copy.wait()
-    done = total_of(a_held2[:, mine_z, :], a_land3)
-    proj_ref[:, :, 0:piece] = done[:, :CAP]
-    proj_ref[:, :, piece : 2 * piece] = done[:, CAP:]
-    for copy in b_copies:
-        copy.wait()
-    done = total_of(b_held2[:, mine_z, :], b_land3)
-    proj_ref[:, :, 2 * piece : 3 * piece] = done[:, :CAP]
-    proj_ref[:, :, 3 * piece :] = done[:, CAP:]
+    for odd, copies, held2, landing in ((0, a_copies, a_held2, a_land3), (1, b_copies, b_held2, b_land3)):
+        for copy in copies:
+            copy.wait()
+        done = total_of(held2[:, z], landing)
+        for turn in range(2):
+            pair = 2 * turn + odd
+            proj_ref[:, :, pair * 2 * DH : (pair + 1) * 2 * DH] = done[
+                :, turn * CAP : (turn + 1) * CAP
+            ]
     wait_bytes(outgoing.at[pl.ds(0, (N - 1) * SLAB)], send_sem)
     wait_bytes(back.at[pl.ds(0, (N - 1) * SLAB)], back_send)
-
 
 def layer(lists, valid, idx, feats, weight, gain, grad):
     rows, width = feats.shape
@@ -512,7 +558,7 @@
     keys = rows + N * CAP
     quarter = width // 4
     piece = cols // 4
-    strip = AZ * SLAB
+    strip = AZ * CAP
     terms = N * SLAB + 2 * rows
     smem = pl.BlockSpec(memory_space=pltpu.SMEM)
     vmem = pl.BlockSpec(memory_space=pltpu.VMEM)
@@ -548,27 +594,25 @@
             ram((heads, 1, rows), F32),
             ram((heads, 1, rows), F32),
             ram((cols, rows), F32),
-            ram((rows, cols), F32),
-            ram((keys, cols), BF16),
-            ram((keys, cols), BF16),
+            ram((heads // 2, keys, 4 * DH), BF16),
             ram((rows, cols), BF16),
-            ram((terms, quarter), F32),
+            ram((2 * rows, quarter), F32),
             ram((terms, quarter), BF16),
             ram((terms, quarter), BF16),
             ram((N * SLAB, quarter), BF16),
             ram((N * SLAB, quarter), BF16),
-            ram((AX, 3, AY, strip, piece), BF16),
-            ram((AY, 3, AX, strip, piece), BF16),
-            ram((AX - 1, 3, AY, strip, piece), BF16),
-            ram((AY - 1, 3, AX, strip, piece), BF16),
-            ram((3, AY, strip, piece), BF16),
-            ram((3, AX, strip, piece), BF16),
-            ram((AY - 1, 3, strip, piece), BF16),
-            ram((AX - 1, 3, strip, piece), BF16),
-            ram((3, strip, piece), BF16),
-            ram((3, strip, piece), BF16),
-            ram((AZ - 1, 3, SLAB, piece), BF16),
-            ram((AZ - 1, 3, SLAB, piece), BF16),
+            ram((2, AX, 3, AY, strip, piece), BF16),
+            ram((2, AY, 3, AX, strip, piece), BF16),
+            ram((2, AX - 1, 3, AY, strip, piece), BF16),
+            ram((2, AY - 1, 3, AX, strip, piece), BF16),
+            ram((2, 3, AY, strip, piece), BF16),
+            ram((2, 3, AX, strip, piece), BF16),
+            ram((2, AY - 1, 3, strip, piece), BF16),
+            ram((2, AX - 1, 3, strip, piece), BF16),
+            ram((3, AZ, 2 * CAP, piece), BF16),
+            ram((3, AZ, 2 * CAP, piece), BF16),
+            ram((AZ - 1, 3, 2 * CAP, piece), BF16),
+            ram((AZ - 1, 3, 2 * CAP, piece), BF16),
             dma,
             dma((AX,)),
             dma((AX,)),
@@ -577,14 +621,14 @@
             dma((AX + 1,)),
             dma,
             dma((AX,)),
-            dma((AX - 1,)),
-            dma((AX - 1,)),
-            dma((AY - 1,)),
-            dma((AY - 1,)),
-            dma((AY - 1,)),
-            dma((AY - 1,)),
-            dma((AX - 1,)),
-            dma((AX - 1,)),
+            dma((2, AX - 1)),
+            dma((2, AX - 1)),
+            dma((2, AY - 1)),
+            dma((2, AY - 1)),
+            dma((2, AY - 1)),
+            dma((2, AY - 1)),
+            dma((2, AX - 1)),
+            dma((2, AX - 1)),
             dma((AZ - 1,)),
             dma((AZ - 1,)),
             dma((AZ - 1,)),

time: 112 us -> 105 us (0.938)
  Pallas kernels: 107 us -> 99.6 us
    pallas_call x1, Pallas kernels: 107 us -> 99.6 us  [layer(): pl.pallas_call(layer_kernel, out_shape=[jax.ShapeDtypeStruct((3, CAP, col...]
where the time goes in v3:
time: 105 us
  Pallas kernels  99.6 us (95%)
  local copies, waits for them, and re-layouts  3.89 us (4%)
    pallas_call x1, Pallas kernels, layer(): pl.pallas_call(layer_kernel, out_shape=[jax.ShapeDtypeStruct((3, CAP, col...  99.6 us
    unnamed x2, local copies, waits for them, and re-layouts  3.09 us

profile of v3, /device:TPU:32, one launch (start us, length us, event | category | flops | bytes accessed | tf_op | source)
XLA Modules:
  0.0 104.8 jit_solution(11416624096025588494)
XLA Ops:
  0.6 0.7 fusion
  1.3 0.1 copy.11
  1.4 0.7 reshape.10.idx_ref
  2.1 99.6 %layer.1 = (f32[3,8,512]{2,1,0:T(8,128)}, bf16[256,512]{1,0:T(8,128)(2,1)}) custom-call(s32[2,6]{1,0:T(2,128)} %lists_ref.1, s32[2]{0:T(128)} %valid_ref.1, s32[4,1,512]{2,1,0:T(1,128)} %reshape.10.idx_ref, bf16[256,1024]{1,0:T(8,128)(2,1)} %feats_ref.1, bf16[3,1024,512]{2,1,0:T(8,128)(2,1)} %bitcast.3, f32[2,512]{1,0:T(2,128)} %gain_ref.1, ...), custom_call_target="tpu_custom_call" | custom-call | tf_op jit(solution)/shard_map/layer/pallas_call | solution.py:567
  101.7 1.4 %copy.15 = f32[8,3,512]{2,0,1:T(8,128)} copy(f32[8,3,512]{2,0,1:T(8,128)} %bitcast.4) | data formatting | bytes 98304
  103.2 1.7 %copy.16 = bf16[256,512]{1,0:T(8,128)(2,1)} copy(bf16[256,512]{1,0:T(8,128)(2,1)} %get-tuple-element.11) | data formatting | bytes 524288
  (1 shorter events, 0.0 us)

commit v4 on v3

--- a/solution.py
+++ b/solution.py
@@ -137,11 +137,13 @@
     valid_ref,
     idx_ref,
     feats_ref,
-    weight_ref,
+    weight_hbm,
     gain_ref,
-    grad_ref,
+    grad_hbm,
     proj_ref,
     input_ref,
+    weight_ref,
+    grad_ref,
     halves,
     outgoing,
     landed,
@@ -163,6 +165,7 @@
     total,
     moment,
     dq_t,
+    slope,
     kv_low,
     dq_low,
     keep,
@@ -202,9 +205,16 @@
     a_recv3,
     b_send3,
     b_recv3,
+    load_sem,
 ):
     mine = place()
     dom, core, x, z, y = mine
+    loads = [
+        pltpu.make_async_copy(weight_hbm, weight_ref, load_sem.at[0]),
+        pltpu.make_async_copy(grad_hbm, grad_ref, load_sem.at[1]),
+    ]
+    for load in loads:
+        load.start()
     barrier = greet_all(dom, core)
     rows, width = feats_ref.shape
     cols = grad_ref.shape[1]
@@ -281,8 +291,8 @@
                     tile_live(j) * listed.astype(F32)
                 )
 
-        def head_pair(pair, carry):
-            lanes = lanes_of(pair)
+        def head_pair(pair):
+            lanes = slice(pair * 2 * DH, (pair + 1) * 2 * DH)
             k_pair = k_hat[part, lanes]
             v_pair = values[part, lanes]
             for h in range(2):
@@ -298,10 +308,12 @@
                 else:
                     total[head] += jnp.sum(e, axis=0, keepdims=True)
                     moment[head] += jnp.sum(e_dp, axis=0, keepdims=True)
-            return carry
-
-        lax.fori_loop(0, heads // 2, head_pair, 0)
-
+
+        for pair in range(heads // 2):
+            head_pair(pair)
+
+    for load in loads:
+        load.wait()
     own_block = feats_ref[...]
     unit, inv = normed(dot(own_block, weight_ref[0]))
     q_inv[...] = inv
@@ -315,12 +327,19 @@
     place_in_tile = lax.broadcasted_iota(jnp.int32, (TILE, TILE), 0)
     consume(0, own_block, lambda j: jnp.where(place_in_tile < valid_ref[j], 1.0, 0.0), 0)
 
-    for step in range(AX):
-        near = lax.rem(x - step + AX, AX)
-        wait_block(step, near, landed.at[core], recv_sem)
-        arrived = landed.at[core, rows_at(near * BLOCK, BLOCK)]
-        pair = to_other_core(arrived, arrived, core, half_send.at[step], half_recv.at[step])
-        pair.wait()
+    swaps = []
+    for step in range(AX + 1):
+        if step < AX:
+            near = lax.rem(x - step + AX, AX)
+            wait_block(step, near, landed.at[core], recv_sem)
+            arrived = landed.at[core, rows_at(near * BLOCK, BLOCK)]
+            swaps.append(
+                to_other_core(arrived, arrived, core, half_send.at[step], half_recv.at[step])
+            )
+        if step == 0:
+            continue
+        near = lax.rem(x - (step - 1) + AX, AX)
+        swaps[step - 1].wait()
         strips = []
         for plane in range(2):
             slabs = landed[plane, rows_at(near * BLOCK, BLOCK), :].astype(F32)
@@ -334,7 +353,7 @@
             return jnp.where(column < LIVE_MAX, 1.0, 0.0)
 
         block = jnp.concatenate([strip.astype(BF16) for strip in strips], axis=1)
-        consume(step + 1, block, received_live, own_tiles + near * own_tiles)
+        consume(step, block, received_live, own_tiles + near * own_tiles)
 
     for head in range(heads):
         lanes = pl.ds(head // 2 * 2 * DH, 2 * DH)
@@ -345,7 +364,6 @@
             which == head % 2, q_t[lanes, :] * (over * (1.0 / LOG2E)), 0.0
         ).astype(BF16)
         g_head[head] = jnp.where(which == head % 2, g_t[lanes, :] * over, 0.0).astype(BF16)
-    dq_t[...] = jnp.zeros(dq_t.shape, F32)
 
     pair_mean = head_mean[: 2 * DH, : 2 * DH]
 
@@ -353,32 +371,33 @@
         inner = dot((unit * upstream).astype(BF16), pair_mean)
         return inv * (upstream - unit * inner)
 
-    def second_pass(pair):
+    def second_pass(pair, b):
         lanes = slice(pair * 2 * DH, (pair + 1) * 2 * DH)
+        part = part_of(b)
+        lows, slopes = [], []
+        for h in range(2):
+            head = pair * 2 + h
+            low = expo[head, part, :]
+            ds = expo_dp[head, part, :] - low.astype(F32) * moment[head]
+            ds = ds.astype(BF16)
+            slope[pair % 2, h, part, :] = ds
+            lows.append(low)
+            slopes.append(ds)
+        g_both = jnp.concatenate([g_head[pair * 2], g_head[pair * 2 + 1]], axis=1)
         q_both = jnp.concatenate([q_head[pair * 2], q_head[pair * 2 + 1]], axis=1)
-        g_both = jnp.concatenate([g_head[pair * 2], g_head[pair * 2 + 1]], axis=1)
-
-        def key_block(b, carry):
-            part = pl.ds(pl.multiple_of(b * rows, rows), rows)
-            lows, slopes = [], []
-            for head in (pair * 2, pair * 2 + 1):
-                low = expo[head, part, :]
-                ds = (expo_dp[head, part, :] - low.astype(F32) * moment[head]).astype(BF16)
-                head_rows = slice(head * DH, (head + 1) * DH)
-                dq_t[head_rows, :] += dot(k_hat_t[head_rows, part], ds)
-                lows.append(low)
-                slopes.append(ds)
-            dv = dot_nt(jnp.concatenate(lows, axis=1), g_both)
-            dk = dot_nt(jnp.concatenate(slopes, axis=1), q_both) * gain_ref[1:2, lanes]
-            dk = norm_back(k_unit[part, lanes], k_inv[part, lanes], dk)
-            kv_low[pair, part, 0 : 2 * DH] = dk.astype(BF16)
-            kv_low[pair, part, 2 * DH :] = dv.astype(BF16)
-            return carry
-
-        lax.fori_loop(0, AX + 1, key_block, 0)
-        for head in (pair * 2, pair * 2 + 1):
+        dv = dot_nt(jnp.concatenate(lows, axis=1), g_both)
+        dk = dot_nt(jnp.concatenate(slopes, axis=1), q_both) * gain_ref[1:2, lanes]
+        dk = norm_back(k_unit[part, lanes], k_inv[part, lanes], dk)
+        kv_low[pair, part, 0 : 2 * DH] = dk.astype(BF16)
+        kv_low[pair, part, 2 * DH :] = dv.astype(BF16)
+
+    def query_terms(pair):
+        lanes = slice(pair * 2 * DH, (pair + 1) * 2 * DH)
+        for h in range(2):
+            head = pair * 2 + h
             head_rows = slice(head * DH, (head + 1) * DH)
-            dq_t[head_rows, :] = dq_t[head_rows, :] * (total[head] * (1.0 / math.sqrt(DH)))
+            dq = dot(k_hat_t[head_rows, :], slope[pair % 2, h])
+            dq_t[head_rows, :] = dq * (total[head] * (1.0 / math.sqrt(DH)))
         upstream = dq_t[lanes, :].T * gain_ref[0:1, lanes]
         dq_low[:, lanes] = norm_back(q_unit[:, lanes], q_inv[:, lanes], upstream).astype(BF16)
 
@@ -428,12 +447,14 @@
             for s in range(1, AY)
         ]
 
-    second_pass(0)
+    for b in range(AX + 1):
+        second_pass(0, b)
+    query_terms(0)
     a_first = gradient_columns(0)
-    second_pass(1)
+    for b in range(AX + 1):
+        second_pass(1, b)
+    query_terms(1)
     b_first = gradient_columns(1)
-    second_pass(2)
-    second_pass(3)
 
     pairs = []
 
@@ -466,10 +487,15 @@
         back[part, :] = (kept + pair_land[local, :].astype(F32)).astype(BF16)
         push_block((AX - step) % AX, mine, back, back_land, back_send, back_recv)
 
-    give_term(0)
-    for step in range(AX):
-        give_term(step + 1)
-        return_term(step)
+    for step in range(AX + 1):
+        second_pass(2, (step + 1) % (AX + 1))
+        second_pass(3, (step + 1) % (AX + 1))
+        if step == AX:
+            query_terms(2)
+            query_terms(3)
+        give_term(step)
+        if step > 0:
+            return_term(step - 1)
     back_land[own_slab, :] = back[own_slab, :]
     a_second = gradient_columns(2)
     b_second = gradient_columns(3)
@@ -562,6 +588,7 @@
     terms = N * SLAB + 2 * rows
     smem = pl.BlockSpec(memory_space=pltpu.SMEM)
     vmem = pl.BlockSpec(memory_space=pltpu.VMEM)
+    hbm = pl.BlockSpec(memory_space=pl.ANY)
     ram = pltpu.VMEM
     dma = pltpu.SemaphoreType.DMA
     return pl.pallas_call(
@@ -570,9 +597,11 @@
             jax.ShapeDtypeStruct((3, CAP, cols), F32),
             jax.ShapeDtypeStruct((rows, half_of(width)), BF16),
         ],
-        in_specs=[smem, smem] + [vmem] * 5,
+        in_specs=[smem, smem, vmem, vmem, hbm, vmem, hbm],
         out_specs=[vmem] * 2,
         scratch_shapes=[
+            ram(weight.shape, BF16),
+            ram(grad.shape, BF16),
             ram((2 * rows + SLAB, quarter), BF16),
             ram((N * SLAB, quarter), BF16),
             ram((2, N * SLAB, quarter), BF16),
@@ -594,6 +623,7 @@
             ram((heads, 1, rows), F32),
             ram((heads, 1, rows), F32),
             ram((cols, rows), F32),
+            ram((2, 2, keys, rows), BF16),
             ram((heads // 2, keys, 4 * DH), BF16),
             ram((rows, cols), BF16),
             ram((2 * rows, quarter), F32),
@@ -633,6 +663,7 @@
             dma((AZ - 1,)),
             dma((AZ - 1,)),
             dma((AZ - 1,)),
+            dma((2,)),
         ],
         compiler_params=pltpu.CompilerParams(
             collective_id=0, has_side_effects=True, vmem_limit_bytes=60 * 1024 * 1024

time: 105 us -> 99.8 us (0.950)
  Pallas kernels: 99.6 us -> 94.3 us
    pallas_call x1, Pallas kernels: 99.6 us -> 94.3 us  [layer(): pl.pallas_call(layer_kernel, out_shape=[jax.ShapeDtypeStruct((3, CAP, col...]
where the time goes in v4:
time: 99.8 us; the launch traced here: 99.5 us
  Pallas kernels  94.3 us (94%)
  local copies, waits for them, and re-layouts  3.89 us (4%)
    pallas_call x1, Pallas kernels, layer(): pl.pallas_call(layer_kernel, out_shape=[jax.ShapeDtypeStruct((3, CAP, col...  94.3 us
    unnamed x2, local copies, waits for them, and re-layouts  3.09 us

profile of v4, /device:TPU:32, one launch (start us, length us, event | category | flops | bytes accessed | tf_op | source)
XLA Modules:
  0.0 99.5 jit_solution(5246916278776487978)
XLA Ops:
  0.6 0.7 fusion
  1.3 0.1 copy.11
  1.4 0.7 reshape.10.idx_ref
  2.1 94.3 %layer.1 = (f32[3,8,512]{2,1,0:T(8,128)}, bf16[256,512]{1,0:T(8,128)(2,1)}) custom-call(s32[2,6]{1,0:T(2,128)} %lists_ref.1, s32[2]{0:T(128)} %valid_ref.1, s32[4,1,512]{2,1,0:T(1,128)} %reshape.10.idx_ref, bf16[256,1024]{1,0:T(8,128)(2,1)} %feats_ref.1, bf16[3,1024,512]{2,1,0:T(8,128)(2,1)} %bitcast.3, f32[2,512]{1,0:T(2,128)} %gain_ref.1, ...), custom_call_target="tpu_custom_call" | custom-call | tf_op jit(solution)/shard_map/layer/pallas_call | solution.py:594
  96.4 1.4 %copy.15 = f32[8,3,512]{2,0,1:T(8,128)} copy(f32[8,3,512]{2,0,1:T(8,128)} %bitcast.4) | data formatting | bytes 98304
  97.9 1.7 %copy.16 = bf16[256,512]{1,0:T(8,128)(2,1)} copy(bf16[256,512]{1,0:T(8,128)(2,1)} %get-tuple-element.11) | data formatting | bytes 524288
  (1 shorter events, 0.0 us)

commit v5 on v4

--- a/solution.py
+++ b/solution.py
@@ -113,16 +113,70 @@
 
 
 def axis_copy(step, src, landing, send_sems, recv_sems, peer):
+    return to_peer(src, landing.at[step - 1], send_sems.at[step - 1], recv_sems.at[step - 1], peer)
+
+
+def to_peer(src, dst, send_sem, recv_sem, peer):
     copy = pltpu.make_async_remote_copy(
         src_ref=src,
-        dst_ref=landing.at[step - 1],
-        send_sem=send_sems.at[step - 1],
-        recv_sem=recv_sems.at[step - 1],
+        dst_ref=dst,
+        send_sem=send_sem,
+        recv_sem=recv_sem,
         device_id={"dom": peer},
         device_id_type=MESH,
     )
     copy.start()
     return copy
+
+
+PASS_UP, DONE_UP, PASS_DOWN, DONE_DOWN, LAST_UP, LAST_DOWN = range(6)
+
+
+def axis_begin(blocks, at, landing, send_sems, recv_sems, peer):
+    middle = blocks.shape[2] // 2
+    left, right = pl.ds(0, middle), pl.ds(middle, middle)
+    copies = {}
+    for kind, block, side, step in (
+        (PASS_UP, 2, left, 1),
+        (PASS_DOWN, 2, right, 3),
+        (DONE_UP, 1, right, 1),
+        (DONE_DOWN, 3, left, 3),
+    ):
+        copies[kind] = to_peer(
+            blocks.at[at(block), :, side],
+            landing.at[kind],
+            send_sems.at[kind],
+            recv_sems.at[kind],
+            peer(step),
+        )
+    return copies
+
+
+def axis_pass(copies, blocks, at, landing, passed, send_sems, recv_sems, peer):
+    middle = blocks.shape[2] // 2
+    left, right = slice(0, middle), slice(middle, 2 * middle)
+    for slot, arrived, kind, side, step in (
+        (0, PASS_UP, LAST_UP, left, 1),
+        (1, PASS_DOWN, LAST_DOWN, right, 3),
+    ):
+        copies[arrived].wait()
+        mine = blocks[at(step), :, side].astype(F32)
+        passed[slot] = (mine + landing[arrived].astype(F32)).astype(BF16)
+        copies[kind] = to_peer(
+            passed.at[slot], landing.at[kind], send_sems.at[kind], recv_sems.at[kind], peer(step)
+        )
+
+
+def axis_end(copies, own_block, landing, held):
+    for kind in (DONE_UP, DONE_DOWN, LAST_UP, LAST_DOWN):
+        copies[kind].wait()
+    middle = own_block.shape[1] // 2
+    for side, first, second in (
+        (slice(0, middle), DONE_DOWN, LAST_UP),
+        (slice(middle, 2 * middle), DONE_UP, LAST_DOWN),
+    ):
+        total = own_block[:, side].astype(F32) + landing[first].astype(F32)
+        held[:, side] = (total + landing[second].astype(F32)).astype(BF16)
 
 
 def total_of(own_part, landing):
@@ -177,6 +231,8 @@
     second,
     a_land,
     b_land,
+    a_passed,
+    b_passed,
     a_held,
     b_held,
     a_land2,
@@ -424,28 +480,36 @@
                     else:
                         second[turn, j, c, i] = tile
         if pair % 2 == 0:
-            return [
-                axis_copy(
-                    s,
-                    first.at[turn, at_x(s)],
-                    a_land.at[turn],
-                    a_send.at[turn],
-                    a_recv.at[turn],
-                    peer_x(s),
-                )
-                for s in range(1, AX)
-            ]
-        return [
-            axis_copy(
-                s,
-                second.at[turn, at_y(s)],
-                b_land.at[turn],
-                b_send.at[turn],
-                b_recv.at[turn],
-                peer_y(s),
+            return axis_begin(
+                first.at[turn], at_x, a_land.at[turn], a_send.at[turn], a_recv.at[turn], peer_x
             )
-            for s in range(1, AY)
-        ]
+        return axis_begin(
+            second.at[turn], at_y, b_land.at[turn], b_send.at[turn], b_recv.at[turn], peer_y
+        )
+
+    def pass_a(turn, copies):
+        axis_pass(
+            copies,
+            first.at[turn],
+            at_x,
+            a_land.at[turn],
+            a_passed.at[turn],
+            a_send.at[turn],
+            a_recv.at[turn],
+            peer_x,
+        )
+
+    def pass_b(turn, copies):
+        axis_pass(
+            copies,
+            second.at[turn],
+            at_y,
+            b_land.at[turn],
+            b_passed.at[turn],
+            b_send.at[turn],
+            b_recv.at[turn],
+            peer_y,
+        )
 
     for b in range(AX + 1):
         second_pass(0, b)
@@ -496,15 +560,17 @@
         give_term(step)
         if step > 0:
             return_term(step - 1)
+        if step == 2:
+            pass_a(0, a_first)
+        if step == 3:
+            pass_b(0, b_first)
     back_land[own_slab, :] = back[own_slab, :]
     a_second = gradient_columns(2)
     b_second = gradient_columns(3)
     keep[...] = term_of(AX, core)
 
     def cross_a(turn, copies):
-        for copy in copies:
-            copy.wait()
-        a_held[turn] = total_of(first[turn, x], a_land.at[turn]).astype(BF16)
+        axis_end(copies, first.at[turn, x], a_land.at[turn], a_held.at[turn])
         return [
             axis_copy(
                 s,
@@ -518,9 +584,7 @@
         ]
 
     def cross_b(turn, copies):
-        for copy in copies:
-            copy.wait()
-        b_held[turn] = total_of(second[turn, y], b_land.at[turn]).astype(BF16)
+        axis_end(copies, second.at[turn, y], b_land.at[turn], b_held.at[turn])
         return [
             axis_copy(
                 s,
@@ -543,6 +607,8 @@
 
     a_first = cross_a(0, a_first)
     b_first = cross_b(0, b_first)
+    pass_a(1, a_second)
+    pass_b(1, b_second)
     a_second = cross_a(1, a_second)
     b_second = cross_b(1, b_second)
     for copy in a_first + a_second:
@@ -633,8 +699,10 @@
             ram((N * SLAB, quarter), BF16),
             ram((2, AX, 3, AY, strip, piece), BF16),
             ram((2, AY, 3, AX, strip, piece), BF16),
-            ram((2, AX - 1, 3, AY, strip, piece), BF16),
-            ram((2, AY - 1, 3, AX, strip, piece), BF16),
+            ram((2, 6, 3, AY // 2, strip, piece), BF16),
+            ram((2, 6, 3, AX // 2, strip, piece), BF16),
+            ram((2, 2, 3, AY // 2, strip, piece), BF16),
+            ram((2, 2, 3, AX // 2, strip, piece), BF16),
             ram((2, 3, AY, strip, piece), BF16),
             ram((2, 3, AX, strip, piece), BF16),
             ram((2, AY - 1, 3, strip, piece), BF16),
@@ -651,10 +719,10 @@
             dma((AX + 1,)),
             dma,
             dma((AX,)),
-            dma((2, AX - 1)),
-            dma((2, AX - 1)),
-            dma((2, AY - 1)),
-            dma((2, AY - 1)),
+            dma((2, 6)),
+            dma((2, 6)),
+            dma((2, 6)),
+            dma((2, 6)),
             dma((2, AY - 1)),
             dma((2, AY - 1)),
             dma((2, AX - 1)),

time: 99.8 us -> 100 us (level)
  no operation moved by 1% of the time
where the time goes in v5:
time: 100 us; the launch traced here: 99.8 us
  Pallas kernels  94.6 us (95%)
  local copies, waits for them, and re-layouts  3.89 us (4%)
    pallas_call x1, Pallas kernels, layer(): pl.pallas_call(layer_kernel, out_shape=[jax.ShapeDtypeStruct((3, CAP, col...  94.6 us
    unnamed x2, local copies, waits for them, and re-layouts  3.09 us

profile of v5, /device:TPU:32, one launch (start us, length us, event | category | flops | bytes accessed | tf_op | source)
XLA Modules:
  0.0 99.8 jit_solution(13389572832399371859)
XLA Ops:
  0.6 0.7 fusion
  1.3 0.1 copy.11
  1.4 0.7 reshape.10.idx_ref
  2.1 94.6 %layer.1 = (f32[3,8,512]{2,1,0:T(8,128)}, bf16[256,512]{1,0:T(8,128)(2,1)}) custom-call(s32[2,6]{1,0:T(2,128)} %lists_ref.1, s32[2]{0:T(128)} %valid_ref.1, s32[4,1,512]{2,1,0:T(1,128)} %reshape.10.idx_ref, bf16[256,1024]{1,0:T(8,128)(2,1)} %feats_ref.1, bf16[3,1024,512]{2,1,0:T(8,128)(2,1)} %bitcast.3, f32[2,512]{1,0:T(2,128)} %gain_ref.1, ...), custom_call_target="tpu_custom_call" | custom-call | tf_op jit(solution)/shard_map/layer/pallas_call | solution.py:660
  96.7 1.4 %copy.15 = f32[8,3,512]{2,0,1:T(8,128)} copy(f32[8,3,512]{2,0,1:T(8,128)} %bitcast.4) | data formatting | bytes 98304
  98.1 1.7 %copy.16 = bf16[256,512]{1,0:T(8,128)(2,1)} copy(bf16[256,512]{1,0:T(8,128)(2,1)} %get-tuple-element.11) | data formatting | bytes 524288
  (1 shorter events, 0.0 us)

commit v6 on v4

--- a/solution.py
+++ b/solution.py
@@ -455,51 +455,14 @@
         second_pass(1, b)
     query_terms(1)
     b_first = gradient_columns(1)
-
-    pairs = []
-
-    def term_of(step, near):
-        part = part_of((step + 1) % (AX + 1))
-        wanted = pl.ds(pl.multiple_of(near * half, half), half)
-        dk = jnp.concatenate([kv_low[p, part, 0 : 2 * DH] for p in range(heads // 2)], axis=1)
-        dv = jnp.concatenate([kv_low[p, part, 2 * DH :] for p in range(heads // 2)], axis=1)
-        term = dot_nt(dk, weight_ref[1, wanted, :]) + dot_nt(dv, weight_ref[2, wanted, :])
-        if step == AX:
-            term += dot_nt(dq_low[...], weight_ref[0, wanted, :])
-            return jnp.concatenate([term[:, :quarter], term[:, quarter:]], axis=0)
-        return slabbed(term, quarter)
-
-    def give_term(step):
-        local = pl.ds(step * BLOCK, BLOCK)
-        give[local, :] = term_of(step, 1 - core).astype(BF16)
-        pairs.append(
-            to_other_core(
-                give.at[local], pair_land.at[local], core, pair_send.at[step], pair_recv.at[step]
-            )
-        )
-
-    def return_term(step):
-        near = lax.rem(x - step + AX, AX)
-        part = rows_at(near * BLOCK, BLOCK)
-        local = pl.ds(step * BLOCK, BLOCK)
-        kept = term_of(step, core)
-        pairs[step].wait()
-        back[part, :] = (kept + pair_land[local, :].astype(F32)).astype(BF16)
-        push_block((AX - step) % AX, mine, back, back_land, back_send, back_recv)
-
-    for step in range(AX + 1):
-        second_pass(2, (step + 1) % (AX + 1))
-        second_pass(3, (step + 1) % (AX + 1))
-        if step == AX:
-            query_terms(2)
-            query_terms(3)
-        give_term(step)
-        if step > 0:
-            return_term(step - 1)
-    back_land[own_slab, :] = back[own_slab, :]
+    for b in range(AX + 1):
+        second_pass(2, b)
+    query_terms(2)
     a_second = gradient_columns(2)
+    for b in range(AX + 1):
+        second_pass(3, b)
+    query_terms(3)
     b_second = gradient_columns(3)
-    keep[...] = term_of(AX, core)
 
     def cross_a(turn, copies):
         for copy in copies:
@@ -541,8 +504,52 @@
             for s in range(1, AZ)
         ]
 
-    a_first = cross_a(0, a_first)
-    b_first = cross_b(0, b_first)
+    pairs = []
+
+    def term_of(step, near):
+        part = part_of((step + 1) % (AX + 1))
+        wanted = pl.ds(pl.multiple_of(near * half, half), half)
+        dk = jnp.concatenate([kv_low[p, part, 0 : 2 * DH] for p in range(heads // 2)], axis=1)
+        dv = jnp.concatenate([kv_low[p, part, 2 * DH :] for p in range(heads // 2)], axis=1)
+        term = dot_nt(dk, weight_ref[1, wanted, :]) + dot_nt(dv, weight_ref[2, wanted, :])
+        if step == AX:
+            term += dot_nt(dq_low[...], weight_ref[0, wanted, :])
+            return jnp.concatenate([term[:, :quarter], term[:, quarter:]], axis=0)
+        return slabbed(term, quarter)
+
+    def give_term(step):
+        local = pl.ds(step * BLOCK, BLOCK)
+        give[local, :] = term_of(step, 1 - core).astype(BF16)
+        pairs.append(
+            to_other_core(
+                give.at[local], pair_land.at[local], core, pair_send.at[step], pair_recv.at[step]
+            )
+        )
+
+    def return_term(step):
+        near = lax.rem(x - step + AX, AX)
+        part = rows_at(near * BLOCK, BLOCK)
+        local = pl.ds(step * BLOCK, BLOCK)
+        kept = term_of(step, core)
+        pairs[step].wait()
+        back[part, :] = (kept + pair_land[local, :].astype(F32)).astype(BF16)
+
+    def push_back(step):
+        push_block((AX - step) % AX, mine, back, back_land, back_send, back_recv)
+
+    for step in range(AX + 1):
+        give_term(step)
+        if step > 0:
+            return_term(step - 1)
+        if step > 0:
+            push_back(step - 1)
+        if step == 2:
+            a_first = cross_a(0, a_first)
+        if step == 3:
+            b_first = cross_b(0, b_first)
+    back_land[own_slab, :] = back[own_slab, :]
+    keep[...] = term_of(AX, core)
+
     a_second = cross_a(1, a_second)
     b_second = cross_b(1, b_second)
     for copy in a_first + a_second:

time: 99.8 us -> 97.5 us (0.977); the launches traced: 99.5 us -> 96.2 us
  Pallas kernels: 94.3 us -> 90.9 us
    pallas_call x1, Pallas kernels: 94.3 us -> 90.9 us  [layer(): pl.pallas_call(layer_kernel, out_shape=[jax.ShapeDtypeStruct((3, CAP, col...]
where the time goes in v6:
time: 97.5 us; the launch traced here: 96.2 us
  Pallas kernels  90.9 us (93%)
  local copies, waits for them, and re-layouts  3.89 us (4%)
    pallas_call x1, Pallas kernels, layer(): pl.pallas_call(layer_kernel, out_shape=[jax.ShapeDtypeStruct((3, CAP, col...  90.9 us
    unnamed x2, local copies, waits for them, and re-layouts  3.09 us

profile of v6, /device:TPU:32, one launch (start us, length us, event | category | flops | bytes accessed | tf_op | source)
XLA Modules:
  0.0 96.2 jit_solution(4192546973269128093)
XLA Ops:
  0.6 0.7 fusion
  1.3 0.1 copy.11
  1.4 0.7 reshape.10.idx_ref
  2.1 90.9 %layer.1 = (f32[3,8,512]{2,1,0:T(8,128)}, bf16[256,512]{1,0:T(8,128)(2,1)}) custom-call(s32[2,6]{1,0:T(2,128)} %lists_ref.1, s32[2]{0:T(128)} %valid_ref.1, s32[4,1,512]{2,1,0:T(1,128)} %reshape.10.idx_ref, bf16[256,1024]{1,0:T(8,128)(2,1)} %feats_ref.1, bf16[3,1024,512]{2,1,0:T(8,128)(2,1)} %bitcast.3, f32[2,512]{1,0:T(2,128)} %gain_ref.1, ...), custom_call_target="tpu_custom_call" | custom-call | tf_op jit(solution)/shard_map/layer/pallas_call | solution.py:601
  93.1 1.4 %copy.15 = f32[8,3,512]{2,0,1:T(8,128)} copy(f32[8,3,512]{2,0,1:T(8,128)} %bitcast.4) | data formatting | bytes 98304
  94.5 1.7 %copy.16 = bf16[256,512]{1,0:T(8,128)(2,1)} copy(bf16[256,512]{1,0:T(8,128)(2,1)} %get-tuple-element.11) | data formatting | bytes 524288
  (1 shorter events, 0.0 us)

commit v7 on v6

--- a/solution.py
+++ b/solution.py
@@ -462,7 +462,6 @@
     for b in range(AX + 1):
         second_pass(3, b)
     query_terms(3)
-    b_second = gradient_columns(3)
 
     def cross_a(turn, copies):
         for copy in copies:
@@ -539,6 +538,8 @@
 
     for step in range(AX + 1):
         give_term(step)
+        if step == 1:
+            b_second = gradient_columns(3)
         if step > 0:
             return_term(step - 1)
         if step > 0:

time: 97.5 us -> 97.8 us (level)
  no operation moved by 1% of the time
where the time goes in v7:
time: 97.8 us; the launch traced here: 96.2 us
  Pallas kernels  91 us (93%)
  local copies, waits for them, and re-layouts  3.89 us (4%)
    pallas_call x1, Pallas kernels, layer(): pl.pallas_call(layer_kernel, out_shape=[jax.ShapeDtypeStruct((3, CAP, col...  91 us
    unnamed x2, local copies, waits for them, and re-layouts  3.09 us

profile of v7, /device:TPU:32, one launch (start us, length us, event | category | flops | bytes accessed | tf_op | source)
XLA Modules:
  0.0 96.2 jit_solution(10547349725608482457)
XLA Ops:
  0.6 0.7 fusion
  1.3 0.1 copy.11
  1.4 0.7 reshape.10.idx_ref
  2.1 91.0 %layer.1 = (f32[3,8,512]{2,1,0:T(8,128)}, bf16[256,512]{1,0:T(8,128)(2,1)}) custom-call(s32[2,6]{1,0:T(2,128)} %lists_ref.1, s32[2]{0:T(128)} %valid_ref.1, s32[4,1,512]{2,1,0:T(1,128)} %reshape.10.idx_ref, bf16[256,1024]{1,0:T(8,128)(2,1)} %feats_ref.1, bf16[3,1024,512]{2,1,0:T(8,128)(2,1)} %bitcast.3, f32[2,512]{1,0:T(2,128)} %gain_ref.1, ...), custom_call_target="tpu_custom_call" | custom-call | tf_op jit(solution)/shard_map/layer/pallas_call | solution.py:602
  93.1 1.4 %copy.15 = f32[8,3,512]{2,0,1:T(8,128)} copy(f32[8,3,512]{2,0,1:T(8,128)} %bitcast.4) | data formatting | bytes 98304
  94.6 1.7 %copy.16 = bf16[256,512]{1,0:T(8,128)(2,1)} copy(bf16[256,512]{1,0:T(8,128)(2,1)} %get-tuple-element.11) | data formatting | bytes 524288
  (1 shorter events, 0.0 us)
